TPU v7x, 128 devices: a whole 4x4x4 slice. The times are simulated.
128 devices in a mesh: row: 8 (over z, x_lo), col: 16 (over x_hi, y, core).
Axes of the slice: x: 4 (x_hi: 2, x_lo: 2; x = x_hi * 2 + x_lo), y: 4, z: 4, core: 2. Of those that a mesh axis runs over, the one named last changes fastest.
Arguments:
- eigen_basis_rows: float32 [16384, 8192], P('row', 'col'), may hold values from -6 to 6
- mirror_entries: float32 [6, 8, 128, 2176], P(None, 'row', 'col'), may hold values from -0.125 to 0.125
- tau_coefficients: float32 [6, 8, 128], P(None, 'row', 'col'), may hold values from 0.5 to 2
- mirror_tallies: int32 [6, 8], P(None, 'row'), may hold values from 32 to 128
Outputs:
- transformed: float32 [16384, 8192], P('row', 'col')
All inputs are finite; a program needn't handle non-finite values.
Results may differ from a plain program's by a relative error of at most 0.00017.
Values sent between devices are 32-bit elements; how exact they have to be, the bound alone decides.
A program may use at most 64 MiB of HBM per device.

v0:
```python
import jax
import jax.numpy as jnp
from jax import lax
from jax.sharding import PartitionSpec as P

PRECISE = lax.Precision.HIGHEST


def shifted(block, axis, distance):
    devices = range(lax.axis_size(axis))
    route = [(i - distance, i) for i in devices if i - distance in devices]
    return lax.ppermute(block, axis, route)


def storage_triangle(mirror_directions, scaling, retention_flags):
    gram_matrix = lax.dot_general(
        mirror_directions,
        mirror_directions,
        (((1,), (1,)), ((), ())),
        precision=PRECISE,
        preferred_element_type=jnp.float32,
    )
    diag_inverse = jnp.where(retention_flags, scaling, jnp.ones_like(scaling))
    nilpotent = diag_inverse[:, None] * jnp.triu(gram_matrix, 1)
    order_count = mirror_directions.shape[0]
    identity = jnp.eye(order_count, dtype=jnp.float32)
    power_term = -nilpotent
    inverse_part = identity + power_term
    reached = 1
    while 2 * reached < order_count:
        power_term = jnp.dot(
            power_term, power_term, precision=PRECISE, preferred_element_type=jnp.float32
        )
        inverse_part = inverse_part + jnp.dot(
            inverse_part, power_term, precision=PRECISE, preferred_element_type=jnp.float32
        )
        reached = reached * 2
    return inverse_part * diag_inverse[None, :]


def apply_block(window, mirror_directions, triangle_operator):
    coeffs = jnp.dot(
        mirror_directions, window, precision=PRECISE, preferred_element_type=jnp.float32
    )
    mixed_terms = jnp.dot(
        triangle_operator, coeffs, precision=PRECISE, preferred_element_type=jnp.float32
    )
    return window - lax.dot_general(
        mirror_directions,
        mixed_terms,
        (((0,), (0,)), ((), ())),
        precision=PRECISE,
        preferred_element_type=jnp.float32,
    )


def per_device(eigen_basis_rows, mirror_entries, tau_coefficients, mirror_tallies):
    gathered, scale_all = (
        lax.all_gather(mirror_entries, "col", axis=2, tiled=True),
        lax.all_gather(tau_coefficients, "col", axis=2, tiled=True),
    )
    householders = gathered[:, 0]
    scale_rows = scale_all[:, 0]
    live_counts = mirror_tallies[:, 0]
    row_count = eigen_basis_rows.shape[0]
    group_count, width_rows, window_rows = householders.shape
    sections = lax.axis_size("row")
    position = lax.axis_index("row")
    slot_index = lax.iota(jnp.int32, width_rows)
    cell_index = lax.iota(jnp.int32, window_rows)
    retention_flags = slot_index[None, :] < live_counts[:, None]
    row_keep = (cell_index < row_count) | (position != sections - 1)
    householders = (
        householders
        * retention_flags[:, :, None].astype(jnp.float32)
        * row_keep[None, None, :].astype(jnp.float32)
    )
    factors = jax.vmap(storage_triangle)(householders, scale_rows, retention_flags)
    total_steps = 2 * (group_count - 1) + sections

    def plan(step_index, panel_ordinal):
        offset = step_index - panel_ordinal
        active = (offset >= 0) & (offset % 2 == 0) & (offset // 2 < group_count)
        return (active, jnp.clip(offset // 2, 0, group_count - 1))

    def advance(step_index, current):
        below_rows = shifted(current[:width_rows], "row", -1)
        active, batch_ordinal = plan(step_index, position)

        def working(state):
            window = jnp.concatenate([state, below_rows], axis=0)
            mirror_directions = lax.dynamic_index_in_dim(
                householders, batch_ordinal, 0, keepdims=False
            )
            triangle_operator = lax.dynamic_index_in_dim(factors, batch_ordinal, 0, keepdims=False)
            updated = apply_block(window, mirror_directions, triangle_operator)
            return (updated[:row_count], updated[row_count:])

        def waiting(state):
            return (state, below_rows)

        current, returned = lax.cond(active, working, waiting, current)
        arrived = shifted(returned, "row", 1)
        sender_active, unused = plan(step_index, position - 1)
        sender_active = sender_active & (position > 0)
        top_rows = jnp.where(sender_active, arrived, current[:width_rows])
        return lax.dynamic_update_slice_in_dim(current, top_rows, 0, 0)

    return lax.fori_loop(0, total_steps, advance, eigen_basis_rows)


def solution(mesh):
    in_specs = (P("row", "col"), P(None, "row", "col", None), P(None, "row", "col"), P(None, "row"))
    out_specs = P("row", "col")
    return jax.shard_map(
        per_device, mesh=mesh, in_specs=in_specs, out_specs=out_specs, check_vma=False
    )
```

profile of v0, /device:TPU:102, one launch (start us, length us, event | category | flops | bytes accessed | tf_op | source)
XLA Modules:
  0.0 707.8 jit_solution(6473481367738353305)
XLA Ops:
  6.5 4.7 copy.26
  11.4 23.0 %all_gather.7 = f32[6,1,128]{0,1,2:T(1,128)S(1)} all-gather(f32[6,1,8]{0,1,2:T(1,128)S(1)} %copy.8), channel_id=1, replica_groups=mesh['row'=8,'col'=16] {'col'}, dimensions={2}, use_global_device_ids=true | all-gather | bytes 3264 | tf_op jit(solution)/shard_map/all_gather | solution.py:60
  34.7 42.0 %all-gather.2.cloned.1.call-done = f32[6,1,128,2176]{3,2,0,1:T(8,128)} async-done(((f32[6,1,8,2176]{3,2,0,1:T(8,128)}), f32[6,1,128,2176]{3,2,0,1:T(8,128)}) %all-gather.2.cloned.1.call-update) | async-done | bytes 6684688 | tf_op jit(solution)/shard_map/all_gather | solution.py:59
  80.3 6.6 fusion.13
  93.4 607.5 %while.16 = (s32[]{:T(128)}, f32[2048,512]{1,0:T(8,128)}, s32[]{:T(128)}, f32[6,128,2176]{2,1,0:T(8,128)}, f32[6,128,128]{2,1,0:T(8,128)S(1)}, /*index=5*/s32[]{...) while((s32[]{:T(128)}, f32[2048,512]{1,0:T(8,128)}, s32[]{:T(128)}, ...), condition=%wide.region_3.4_spmd, body=%wide.region_0.3_spmd.sunk | while | flops 3524395008 | bytes 38470408 | solution.py:109
  96.4 5.9 collective-permute-done
  104.6 9.0 %collective-permute-done.1 = f32[128,512]{1,0:T(8,128)S(1)} collective-permute-done((f32[128,512]{1,0:T(8,128)S(1)}, f32[128,512]{1,0:T(8,128)S(1)}, u32[]{:S(2)}, u32[]{:S(2)}) %collective-permute-start.1) | collective-permute-done | bytes 262176 | tf_op jit(solution)/shard_map/while/body/eval_jaxpr/ppermute | solution.py:12
  115.3 5.1 collective-permute-start
  120.4 4.5 collective-permute-done
  127.2 7.4 %collective-permute-done.1 = f32[128,512]{1,0:T(8,128)S(1)} collective-permute-done((f32[128,512]{1,0:T(8,128)S(1)}, f32[128,512]{1,0:T(8,128)S(1)}, u32[]{:S(2)}, u32[]{:S(2)}) %collective-permute-start.1) | collective-permute-done | bytes 262176 | tf_op jit(solution)/shard_map/while/body/eval_jaxpr/ppermute | solution.py:12
  136.4 4.8 collective-permute-start
  147.4 7.4 %collective-permute-done.1 = f32[128,512]{1,0:T(8,128)S(1)} collective-permute-done((f32[128,512]{1,0:T(8,128)S(1)}, f32[128,512]{1,0:T(8,128)S(1)}, u32[]{:S(2)}, u32[]{:S(2)}) %collective-permute-start.1) | collective-permute-done | bytes 262176 | tf_op jit(solution)/shard_map/while/body/eval_jaxpr/ppermute | solution.py:12
  156.5 4.8 collective-permute-start
  167.5 12.9 %collective-permute-done.1 = f32[128,512]{1,0:T(8,128)S(1)} collective-permute-done((f32[128,512]{1,0:T(8,128)S(1)}, f32[128,512]{1,0:T(8,128)S(1)}, u32[]{:S(2)}, u32[]{:S(2)}) %collective-permute-start.1) | collective-permute-done | bytes 262176 | tf_op jit(solution)/shard_map/while/body/eval_jaxpr/ppermute | solution.py:12
  182.1 18.7 %collective-permute-start = (f32[128,512]{1,0:T(8,128)S(1)}, f32[128,512]{1,0:T(8,128)S(1)}, u32[]{:S(2)}, u32[]{:S(2)}) collective-permute-start(f32[128,512]{1,0:T(8,128)S(1)} %slice.40), channel_id=1, source_target_pairs={{16,0},{32,16},{48,32},{64,48},{80,64},{96,80},{112,96},{17,1},{33... | collective-permute-start | bytes 786440 | tf_op jit(solution)/shard_map/while/body/eval_jaxpr/ppermute | solution.py:12
  200.9 3.8 collective-permute-done
  207.0 23.1 %collective-permute-done.1 = f32[128,512]{1,0:T(8,128)S(1)} collective-permute-done((f32[128,512]{1,0:T(8,128)S(1)}, f32[128,512]{1,0:T(8,128)S(1)}, u32[]{:S(2)}, u32[]{:S(2)}) %collective-permute-start.1) | collective-permute-done | bytes 262176 | tf_op jit(solution)/shard_map/while/body/eval_jaxpr/ppermute | solution.py:12
  231.8 18.0 %collective-permute-start = (f32[128,512]{1,0:T(8,128)S(1)}, f32[128,512]{1,0:T(8,128)S(1)}, u32[]{:S(2)}, u32[]{:S(2)}) collective-permute-start(f32[128,512]{1,0:T(8,128)S(1)} %slice.40), channel_id=1, source_target_pairs={{16,0},{32,16},{48,32},{64,48},{80,64},{96,80},{112,96},{17,1},{33... | collective-permute-start | bytes 786440 | tf_op jit(solution)/shard_map/while/body/eval_jaxpr/ppermute | solution.py:12
  256.0 23.2 %collective-permute-done.1 = f32[128,512]{1,0:T(8,128)S(1)} collective-permute-done((f32[128,512]{1,0:T(8,128)S(1)}, f32[128,512]{1,0:T(8,128)S(1)}, u32[]{:S(2)}, u32[]{:S(2)}) %collective-permute-start.1) | collective-permute-done | bytes 262176 | tf_op jit(solution)/shard_map/while/body/eval_jaxpr/ppermute | solution.py:12
  280.9 19.2 %collective-permute-start = (f32[128,512]{1,0:T(8,128)S(1)}, f32[128,512]{1,0:T(8,128)S(1)}, u32[]{:S(2)}, u32[]{:S(2)}) collective-permute-start(f32[128,512]{1,0:T(8,128)S(1)} %slice.40), channel_id=1, source_target_pairs={{16,0},{32,16},{48,32},{64,48},{80,64},{96,80},{112,96},{17,1},{33... | collective-permute-start | bytes 786440 | tf_op jit(solution)/shard_map/while/body/eval_jaxpr/ppermute | solution.py:12
  306.2 20.8 %collective-permute-done.1 = f32[128,512]{1,0:T(8,128)S(1)} collective-permute-done((f32[128,512]{1,0:T(8,128)S(1)}, f32[128,512]{1,0:T(8,128)S(1)}, u32[]{:S(2)}, u32[]{:S(2)}) %collective-permute-start.1) | collective-permute-done | bytes 262176 | tf_op jit(solution)/shard_map/while/body/eval_jaxpr/ppermute | solution.py:12
  328.8 4.8 collective-permute-start
  337.5 14.4 %conditional.2 = (f32[2048,512]{1,0:T(8,128)}, f32[128,512]{1,0:T(8,128)S(1)}, f32[128,512]{1,0:T(8,128)S(1)}) conditional(s32[]{:T(128)} %convert_element_type.41, (f32[2048,512]{1,0:T(8,128)}, f32[128,512]{1,0:T(8,128)S(1)}) %tuple.59, (f32[2048,512]{1,0:T(8,128)}, f32[128,512]{1,0:T(8,128)S(1)}, s32[]{:T(128)}, f32[6,128,2176]{2,1,0:T(8,128)}, ...), branch_computations={%region_1.1_spmd, %region_2.2_spmd} | conditional | flops 3524329472 | bytes 35061820 | solution.py:102
  340.1 3.9 fusion.1
  344.4 5.0 convolution_subtract_fusion
  353.2 6.9 collective-permute-done.1
  361.8 4.5 collective-permute-start
  366.4 3.8 collective-permute-done
  372.5 21.5 %collective-permute-done.1 = f32[128,512]{1,0:T(8,128)S(1)} collective-permute-done((f32[128,512]{1,0:T(8,128)S(1)}, f32[128,512]{1,0:T(8,128)S(1)}, u32[]{:S(2)}, u32[]{:S(2)}) %collective-permute-start.1) | collective-permute-done | bytes 262176 | tf_op jit(solution)/shard_map/while/body/eval_jaxpr/ppermute | solution.py:12
  395.7 4.8 collective-permute-start
  404.4 14.4 %conditional.2 = (f32[2048,512]{1,0:T(8,128)}, f32[128,512]{1,0:T(8,128)S(1)}, f32[128,512]{1,0:T(8,128)S(1)}) conditional(s32[]{:T(128)} %convert_element_type.41, (f32[2048,512]{1,0:T(8,128)}, f32[128,512]{1,0:T(8,128)S(1)}) %tuple.59, (f32[2048,512]{1,0:T(8,128)}, f32[128,512]{1,0:T(8,128)S(1)}, s32[]{:T(128)}, f32[6,128,2176]{2,1,0:T(8,128)}, ...), branch_computations={%region_1.1_spmd, %region_2.2_spmd} | conditional | flops 3524329472 | bytes 35061820 | solution.py:102
  407.1 3.9 fusion.1
  411.4 5.0 convolution_subtract_fusion
  420.2 6.9 collective-permute-done.1
  428.8 6.0 collective-permute-start
  441.0 20.8 %collective-permute-done.1 = f32[128,512]{1,0:T(8,128)S(1)} collective-permute-done((f32[128,512]{1,0:T(8,128)S(1)}, f32[128,512]{1,0:T(8,128)S(1)}, u32[]{:S(2)}, u32[]{:S(2)}) %collective-permute-start.1) | collective-permute-done | bytes 262176 | tf_op jit(solution)/shard_map/while/body/eval_jaxpr/ppermute | solution.py:12
  463.5 4.8 collective-permute-start
  472.2 14.4 %conditional.2 = (f32[2048,512]{1,0:T(8,128)}, f32[128,512]{1,0:T(8,128)S(1)}, f32[128,512]{1,0:T(8,128)S(1)}) conditional(s32[]{:T(128)} %convert_element_type.41, (f32[2048,512]{1,0:T(8,128)}, f32[128,512]{1,0:T(8,128)S(1)}) %tuple.59, (f32[2048,512]{1,0:T(8,128)}, f32[128,512]{1,0:T(8,128)S(1)}, s32[]{:T(128)}, f32[6,128,2176]{2,1,0:T(8,128)}, ...), branch_computations={%region_1.1_spmd, %region_2.2_spmd} | conditional | flops 3524329472 | bytes 35061820 | solution.py:102
  474.9 3.9 fusion.1
  479.2 5.0 convolution_subtract_fusion
  488.0 6.9 collective-permute-done.1
  496.6 4.3 collective-permute-start
  500.9 3.8 collective-permute-done
  507.1 20.8 %collective-permute-done.1 = f32[128,512]{1,0:T(8,128)S(1)} collective-permute-done((f32[128,512]{1,0:T(8,128)S(1)}, f32[128,512]{1,0:T(8,128)S(1)}, u32[]{:S(2)}, u32[]{:S(2)}) %collective-permute-start.1) | collective-permute-done | bytes 262176 | tf_op jit(solution)/shard_map/while/body/eval_jaxpr/ppermute | solution.py:12
  529.6 4.8 collective-permute-start
  534.5 4.1 collective-permute-done
  538.6 14.4 %conditional.2 = (f32[2048,512]{1,0:T(8,128)}, f32[128,512]{1,0:T(8,128)S(1)}, f32[128,512]{1,0:T(8,128)S(1)}) conditional(s32[]{:T(128)} %convert_element_type.41, (f32[2048,512]{1,0:T(8,128)}, f32[128,512]{1,0:T(8,128)S(1)}) %tuple.59, (f32[2048,512]{1,0:T(8,128)}, f32[128,512]{1,0:T(8,128)S(1)}, s32[]{:T(128)}, f32[6,128,2176]{2,1,0:T(8,128)}, ...), branch_computations={%region_1.1_spmd, %region_2.2_spmd} | conditional | flops 3524329472 | bytes 35061820 | solution.py:102
  541.2 3.9 fusion.1
  545.5 5.0 convolution_subtract_fusion
  554.3 7.5 %collective-permute-done.1 = f32[128,512]{1,0:T(8,128)S(1)} collective-permute-done((f32[128,512]{1,0:T(8,128)S(1)}, f32[128,512]{1,0:T(8,128)S(1)}, u32[]{:S(2)}, u32[]{:S(2)}) %collective-permute-start.1) | collective-permute-done | bytes 262176 | tf_op jit(solution)/shard_map/while/body/eval_jaxpr/ppermute | solution.py:12
  566.0 4.0 collective-permute-done
  572.4 24.8 %collective-permute-done.1 = f32[128,512]{1,0:T(8,128)S(1)} collective-permute-done((f32[128,512]{1,0:T(8,128)S(1)}, f32[128,512]{1,0:T(8,128)S(1)}, u32[]{:S(2)}, u32[]{:S(2)}) %collective-permute-start.1) | collective-permute-done | bytes 262176 | tf_op jit(solution)/shard_map/while/body/eval_jaxpr/ppermute | solution.py:12
  601.7 5.6 collective-permute-done
  607.3 14.4 %conditional.2 = (f32[2048,512]{1,0:T(8,128)}, f32[128,512]{1,0:T(8,128)S(1)}, f32[128,512]{1,0:T(8,128)S(1)}) conditional(s32[]{:T(128)} %convert_element_type.41, (f32[2048,512]{1,0:T(8,128)}, f32[128,512]{1,0:T(8,128)S(1)}) %tuple.59, (f32[2048,512]{1,0:T(8,128)}, f32[128,512]{1,0:T(8,128)S(1)}, s32[]{:T(128)}, f32[6,128,2176]{2,1,0:T(8,128)}, ...), branch_computations={%region_1.1_spmd, %region_2.2_spmd} | conditional | flops 3524329472 | bytes 35061820 | solution.py:102
  610.0 3.9 fusion.1
  614.2 5.0 convolution_subtract_fusion
  623.1 9.0 %collective-permute-done.1 = f32[128,512]{1,0:T(8,128)S(1)} collective-permute-done((f32[128,512]{1,0:T(8,128)S(1)}, f32[128,512]{1,0:T(8,128)S(1)}, u32[]{:S(2)}, u32[]{:S(2)}) %collective-permute-start.1) | collective-permute-done | bytes 262176 | tf_op jit(solution)/shard_map/while/body/eval_jaxpr/ppermute | solution.py:12
  633.8 6.3 collective-permute-start
  646.3 20.8 %collective-permute-done.1 = f32[128,512]{1,0:T(8,128)S(1)} collective-permute-done((f32[128,512]{1,0:T(8,128)S(1)}, f32[128,512]{1,0:T(8,128)S(1)}, u32[]{:S(2)}, u32[]{:S(2)}) %collective-permute-start.1) | collective-permute-done | bytes 262176 | tf_op jit(solution)/shard_map/while/body/eval_jaxpr/ppermute | solution.py:12
  668.9 4.8 collective-permute-start
  677.5 14.4 %conditional.2 = (f32[2048,512]{1,0:T(8,128)}, f32[128,512]{1,0:T(8,128)S(1)}, f32[128,512]{1,0:T(8,128)S(1)}) conditional(s32[]{:T(128)} %convert_element_type.41, (f32[2048,512]{1,0:T(8,128)}, f32[128,512]{1,0:T(8,128)S(1)}) %tuple.59, (f32[2048,512]{1,0:T(8,128)}, f32[128,512]{1,0:T(8,128)S(1)}, s32[]{:T(128)}, f32[6,128,2176]{2,1,0:T(8,128)}, ...), branch_computations={%region_1.1_spmd, %region_2.2_spmd} | conditional | flops 3524329472 | bytes 35061820 | solution.py:102
  680.2 3.9 fusion.1
  684.5 5.0 convolution_subtract_fusion
  693.3 6.9 collective-permute-done.1
  (152 shorter events, 165.9 us)
Async XLA Ops:
  6.5 4.7 copy-start.1
  6.5 4.8 copy-start.2
  6.5 70.2 %all-gather.2.cloned.1.call-start = ((), (), s32[]{:S(2)}) async-start(), calls=%async_computation | async-start | bytes 7102464 | tf_op jit(solution)/shard_map/all_gather | solution.py:59
  80.2 6.6 copy-start
  94.4 7.8 %collective-permute-start = (f32[128,512]{1,0:T(8,128)S(1)}, f32[128,512]{1,0:T(8,128)S(1)}, u32[]{:S(2)}, u32[]{:S(2)}) collective-permute-start(f32[128,512]{1,0:T(8,128)S(1)} %slice.40), channel_id=1, source_target_pairs={{16,0},{32,16},{48,32},{64,48},{80,64},{96,80},{112,96},{17,1},{33... | collective-permute-start | bytes 786440 | tf_op jit(solution)/shard_map/while/body/eval_jaxpr/ppermute | solution.py:12
  103.3 10.3 %collective-permute-start.1 = (f32[128,512]{1,0:T(8,128)S(1)}, f32[128,512]{1,0:T(8,128)S(1)}, u32[]{:S(2)}, u32[]{:S(2)}) collective-permute-start(f32[128,512]{1,0:T(8,128)S(1)} %get-tuple-element.288), channel_id=1, source_target_pairs={{0,16},{16,32},{32,48},{48,64},{64,80},{80,96},{96,112},{1,17},{17... | collective-permute-start | bytes 786440 | tf_op jit(solution)/shard_map/while/body/eval_jaxpr/ppermute | solution.py:12
  115.3 9.6 %collective-permute-start = (f32[128,512]{1,0:T(8,128)S(1)}, f32[128,512]{1,0:T(8,128)S(1)}, u32[]{:S(2)}, u32[]{:S(2)}) collective-permute-start(f32[128,512]{1,0:T(8,128)S(1)} %slice.40), channel_id=1, source_target_pairs={{16,0},{32,16},{48,32},{64,48},{80,64},{96,80},{112,96},{17,1},{33... | collective-permute-start | bytes 786440 | tf_op jit(solution)/shard_map/while/body/eval_jaxpr/ppermute | solution.py:12
  125.9 8.8 %collective-permute-start.1 = (f32[128,512]{1,0:T(8,128)S(1)}, f32[128,512]{1,0:T(8,128)S(1)}, u32[]{:S(2)}, u32[]{:S(2)}) collective-permute-start(f32[128,512]{1,0:T(8,128)S(1)} %get-tuple-element.288), channel_id=1, source_target_pairs={{0,16},{16,32},{32,48},{48,64},{64,80},{80,96},{96,112},{1,17},{17... | collective-permute-start | bytes 786440 | tf_op jit(solution)/shard_map/while/body/eval_jaxpr/ppermute | solution.py:12
  136.4 8.7 %collective-permute-start = (f32[128,512]{1,0:T(8,128)S(1)}, f32[128,512]{1,0:T(8,128)S(1)}, u32[]{:S(2)}, u32[]{:S(2)}) collective-permute-start(f32[128,512]{1,0:T(8,128)S(1)} %slice.40), channel_id=1, source_target_pairs={{16,0},{32,16},{48,32},{64,48},{80,64},{96,80},{112,96},{17,1},{33... | collective-permute-start | bytes 786440 | tf_op jit(solution)/shard_map/while/body/eval_jaxpr/ppermute | solution.py:12
  146.0 8.7 %collective-permute-start.1 = (f32[128,512]{1,0:T(8,128)S(1)}, f32[128,512]{1,0:T(8,128)S(1)}, u32[]{:S(2)}, u32[]{:S(2)}) collective-permute-start(f32[128,512]{1,0:T(8,128)S(1)} %get-tuple-element.288), channel_id=1, source_target_pairs={{0,16},{16,32},{32,48},{48,64},{64,80},{80,96},{96,112},{1,17},{17... | collective-permute-start | bytes 786440 | tf_op jit(solution)/shard_map/while/body/eval_jaxpr/ppermute | solution.py:12
  156.5 8.7 %collective-permute-start = (f32[128,512]{1,0:T(8,128)S(1)}, f32[128,512]{1,0:T(8,128)S(1)}, u32[]{:S(2)}, u32[]{:S(2)}) collective-permute-start(f32[128,512]{1,0:T(8,128)S(1)} %slice.40), channel_id=1, source_target_pairs={{16,0},{32,16},{48,32},{64,48},{80,64},{96,80},{112,96},{17,1},{33... | collective-permute-start | bytes 786440 | tf_op jit(solution)/shard_map/while/body/eval_jaxpr/ppermute | solution.py:12
  166.1 14.2 %collective-permute-start.1 = (f32[128,512]{1,0:T(8,128)S(1)}, f32[128,512]{1,0:T(8,128)S(1)}, u32[]{:S(2)}, u32[]{:S(2)}) collective-permute-start(f32[128,512]{1,0:T(8,128)S(1)} %get-tuple-element.288), channel_id=1, source_target_pairs={{0,16},{16,32},{32,48},{48,64},{64,80},{80,96},{96,112},{1,17},{17... | collective-permute-start | bytes 786440 | tf_op jit(solution)/shard_map/while/body/eval_jaxpr/ppermute | solution.py:12
  182.1 22.6 %collective-permute-start = (f32[128,512]{1,0:T(8,128)S(1)}, f32[128,512]{1,0:T(8,128)S(1)}, u32[]{:S(2)}, u32[]{:S(2)}) collective-permute-start(f32[128,512]{1,0:T(8,128)S(1)} %slice.40), channel_id=1, source_target_pairs={{16,0},{32,16},{48,32},{64,48},{80,64},{96,80},{112,96},{17,1},{33... | collective-permute-start | bytes 786440 | tf_op jit(solution)/shard_map/while/body/eval_jaxpr/ppermute | solution.py:12
  205.7 24.4 %collective-permute-start.1 = (f32[128,512]{1,0:T(8,128)S(1)}, f32[128,512]{1,0:T(8,128)S(1)}, u32[]{:S(2)}, u32[]{:S(2)}) collective-permute-start(f32[128,512]{1,0:T(8,128)S(1)} %get-tuple-element.288), channel_id=1, source_target_pairs={{0,16},{16,32},{32,48},{48,64},{64,80},{80,96},{96,112},{1,17},{17... | collective-permute-start | bytes 786440 | tf_op jit(solution)/shard_map/while/body/eval_jaxpr/ppermute | solution.py:12
  231.8 21.9 %collective-permute-start = (f32[128,512]{1,0:T(8,128)S(1)}, f32[128,512]{1,0:T(8,128)S(1)}, u32[]{:S(2)}, u32[]{:S(2)}) collective-permute-start(f32[128,512]{1,0:T(8,128)S(1)} %slice.40), channel_id=1, source_target_pairs={{16,0},{32,16},{48,32},{64,48},{80,64},{96,80},{112,96},{17,1},{33... | collective-permute-start | bytes 786440 | tf_op jit(solution)/shard_map/while/body/eval_jaxpr/ppermute | solution.py:12
  254.6 24.5 %collective-permute-start.1 = (f32[128,512]{1,0:T(8,128)S(1)}, f32[128,512]{1,0:T(8,128)S(1)}, u32[]{:S(2)}, u32[]{:S(2)}) collective-permute-start(f32[128,512]{1,0:T(8,128)S(1)} %get-tuple-element.288), channel_id=1, source_target_pairs={{0,16},{16,32},{32,48},{48,64},{64,80},{80,96},{96,112},{1,17},{17... | collective-permute-start | bytes 786440 | tf_op jit(solution)/shard_map/while/body/eval_jaxpr/ppermute | solution.py:12
  280.9 23.0 %collective-permute-start = (f32[128,512]{1,0:T(8,128)S(1)}, f32[128,512]{1,0:T(8,128)S(1)}, u32[]{:S(2)}, u32[]{:S(2)}) collective-permute-start(f32[128,512]{1,0:T(8,128)S(1)} %slice.40), channel_id=1, source_target_pairs={{16,0},{32,16},{48,32},{64,48},{80,64},{96,80},{112,96},{17,1},{33... | collective-permute-start | bytes 786440 | tf_op jit(solution)/shard_map/while/body/eval_jaxpr/ppermute | solution.py:12
  304.9 22.1 %collective-permute-start.1 = (f32[128,512]{1,0:T(8,128)S(1)}, f32[128,512]{1,0:T(8,128)S(1)}, u32[]{:S(2)}, u32[]{:S(2)}) collective-permute-start(f32[128,512]{1,0:T(8,128)S(1)} %get-tuple-element.288), channel_id=1, source_target_pairs={{0,16},{16,32},{32,48},{48,64},{64,80},{80,96},{96,112},{1,17},{17... | collective-permute-start | bytes 786440 | tf_op jit(solution)/shard_map/while/body/eval_jaxpr/ppermute | solution.py:12
  328.8 8.7 %collective-permute-start = (f32[128,512]{1,0:T(8,128)S(1)}, f32[128,512]{1,0:T(8,128)S(1)}, u32[]{:S(2)}, u32[]{:S(2)}) collective-permute-start(f32[128,512]{1,0:T(8,128)S(1)} %slice.40), channel_id=1, source_target_pairs={{16,0},{32,16},{48,32},{64,48},{80,64},{96,80},{112,96},{17,1},{33... | collective-permute-start | bytes 786440 | tf_op jit(solution)/shard_map/while/body/eval_jaxpr/ppermute | solution.py:12
  351.9 8.3 %collective-permute-start.1 = (f32[128,512]{1,0:T(8,128)S(1)}, f32[128,512]{1,0:T(8,128)S(1)}, u32[]{:S(2)}, u32[]{:S(2)}) collective-permute-start(f32[128,512]{1,0:T(8,128)S(1)} %get-tuple-element.288), channel_id=1, source_target_pairs={{0,16},{16,32},{32,48},{48,64},{64,80},{80,96},{96,112},{1,17},{17... | collective-permute-start | bytes 786440 | tf_op jit(solution)/shard_map/while/body/eval_jaxpr/ppermute | solution.py:12
  361.8 8.4 %collective-permute-start = (f32[128,512]{1,0:T(8,128)S(1)}, f32[128,512]{1,0:T(8,128)S(1)}, u32[]{:S(2)}, u32[]{:S(2)}) collective-permute-start(f32[128,512]{1,0:T(8,128)S(1)} %slice.40), channel_id=1, source_target_pairs={{16,0},{32,16},{48,32},{64,48},{80,64},{96,80},{112,96},{17,1},{33... | collective-permute-start | bytes 786440 | tf_op jit(solution)/shard_map/while/body/eval_jaxpr/ppermute | solution.py:12
  371.2 22.9 %collective-permute-start.1 = (f32[128,512]{1,0:T(8,128)S(1)}, f32[128,512]{1,0:T(8,128)S(1)}, u32[]{:S(2)}, u32[]{:S(2)}) collective-permute-start(f32[128,512]{1,0:T(8,128)S(1)} %get-tuple-element.288), channel_id=1, source_target_pairs={{0,16},{16,32},{32,48},{48,64},{64,80},{80,96},{96,112},{1,17},{17... | collective-permute-start | bytes 786440 | tf_op jit(solution)/shard_map/while/body/eval_jaxpr/ppermute | solution.py:12
  395.7 8.7 %collective-permute-start = (f32[128,512]{1,0:T(8,128)S(1)}, f32[128,512]{1,0:T(8,128)S(1)}, u32[]{:S(2)}, u32[]{:S(2)}) collective-permute-start(f32[128,512]{1,0:T(8,128)S(1)} %slice.40), channel_id=1, source_target_pairs={{16,0},{32,16},{48,32},{64,48},{80,64},{96,80},{112,96},{17,1},{33... | collective-permute-start | bytes 786440 | tf_op jit(solution)/shard_map/while/body/eval_jaxpr/ppermute | solution.py:12
  418.8 8.3 %collective-permute-start.1 = (f32[128,512]{1,0:T(8,128)S(1)}, f32[128,512]{1,0:T(8,128)S(1)}, u32[]{:S(2)}, u32[]{:S(2)}) collective-permute-start(f32[128,512]{1,0:T(8,128)S(1)} %get-tuple-element.288), channel_id=1, source_target_pairs={{0,16},{16,32},{32,48},{48,64},{64,80},{80,96},{96,112},{1,17},{17... | collective-permute-start | bytes 786440 | tf_op jit(solution)/shard_map/while/body/eval_jaxpr/ppermute | solution.py:12
  428.8 9.9 %collective-permute-start = (f32[128,512]{1,0:T(8,128)S(1)}, f32[128,512]{1,0:T(8,128)S(1)}, u32[]{:S(2)}, u32[]{:S(2)}) collective-permute-start(f32[128,512]{1,0:T(8,128)S(1)} %slice.40), channel_id=1, source_target_pairs={{16,0},{32,16},{48,32},{64,48},{80,64},{96,80},{112,96},{17,1},{33... | collective-permute-start | bytes 786440 | tf_op jit(solution)/shard_map/while/body/eval_jaxpr/ppermute | solution.py:12
  439.7 22.2 %collective-permute-start.1 = (f32[128,512]{1,0:T(8,128)S(1)}, f32[128,512]{1,0:T(8,128)S(1)}, u32[]{:S(2)}, u32[]{:S(2)}) collective-permute-start(f32[128,512]{1,0:T(8,128)S(1)} %get-tuple-element.288), channel_id=1, source_target_pairs={{0,16},{16,32},{32,48},{48,64},{64,80},{80,96},{96,112},{1,17},{17... | collective-permute-start | bytes 786440 | tf_op jit(solution)/shard_map/while/body/eval_jaxpr/ppermute | solution.py:12
  463.5 8.7 %collective-permute-start = (f32[128,512]{1,0:T(8,128)S(1)}, f32[128,512]{1,0:T(8,128)S(1)}, u32[]{:S(2)}, u32[]{:S(2)}) collective-permute-start(f32[128,512]{1,0:T(8,128)S(1)} %slice.40), channel_id=1, source_target_pairs={{16,0},{32,16},{48,32},{64,48},{80,64},{96,80},{112,96},{17,1},{33... | collective-permute-start | bytes 786440 | tf_op jit(solution)/shard_map/while/body/eval_jaxpr/ppermute | solution.py:12
  486.6 8.3 %collective-permute-start.1 = (f32[128,512]{1,0:T(8,128)S(1)}, f32[128,512]{1,0:T(8,128)S(1)}, u32[]{:S(2)}, u32[]{:S(2)}) collective-permute-start(f32[128,512]{1,0:T(8,128)S(1)} %get-tuple-element.288), channel_id=1, source_target_pairs={{0,16},{16,32},{32,48},{48,64},{64,80},{80,96},{96,112},{1,17},{17... | collective-permute-start | bytes 786440 | tf_op jit(solution)/shard_map/while/body/eval_jaxpr/ppermute | solution.py:12
  496.6 8.2 %collective-permute-start = (f32[128,512]{1,0:T(8,128)S(1)}, f32[128,512]{1,0:T(8,128)S(1)}, u32[]{:S(2)}, u32[]{:S(2)}) collective-permute-start(f32[128,512]{1,0:T(8,128)S(1)} %slice.40), channel_id=1, source_target_pairs={{16,0},{32,16},{48,32},{64,48},{80,64},{96,80},{112,96},{17,1},{33... | collective-permute-start | bytes 786440 | tf_op jit(solution)/shard_map/while/body/eval_jaxpr/ppermute | solution.py:12
  505.8 22.2 %collective-permute-start.1 = (f32[128,512]{1,0:T(8,128)S(1)}, f32[128,512]{1,0:T(8,128)S(1)}, u32[]{:S(2)}, u32[]{:S(2)}) collective-permute-start(f32[128,512]{1,0:T(8,128)S(1)} %get-tuple-element.288), channel_id=1, source_target_pairs={{0,16},{16,32},{32,48},{48,64},{64,80},{80,96},{96,112},{1,17},{17... | collective-permute-start | bytes 786440 | tf_op jit(solution)/shard_map/while/body/eval_jaxpr/ppermute | solution.py:12
  529.6 8.9 %collective-permute-start = (f32[128,512]{1,0:T(8,128)S(1)}, f32[128,512]{1,0:T(8,128)S(1)}, u32[]{:S(2)}, u32[]{:S(2)}) collective-permute-start(f32[128,512]{1,0:T(8,128)S(1)} %slice.40), channel_id=1, source_target_pairs={{16,0},{32,16},{48,32},{64,48},{80,64},{96,80},{112,96},{17,1},{33... | collective-permute-start | bytes 786440 | tf_op jit(solution)/shard_map/while/body/eval_jaxpr/ppermute | solution.py:12
  553.0 8.8 %collective-permute-start.1 = (f32[128,512]{1,0:T(8,128)S(1)}, f32[128,512]{1,0:T(8,128)S(1)}, u32[]{:S(2)}, u32[]{:S(2)}) collective-permute-start(f32[128,512]{1,0:T(8,128)S(1)} %get-tuple-element.288), channel_id=1, source_target_pairs={{0,16},{16,32},{32,48},{48,64},{64,80},{80,96},{96,112},{1,17},{17... | collective-permute-start | bytes 786440 | tf_op jit(solution)/shard_map/while/body/eval_jaxpr/ppermute | solution.py:12
  563.5 6.6 collective-permute-start
  571.1 26.1 %collective-permute-start.1 = (f32[128,512]{1,0:T(8,128)S(1)}, f32[128,512]{1,0:T(8,128)S(1)}, u32[]{:S(2)}, u32[]{:S(2)}) collective-permute-start(f32[128,512]{1,0:T(8,128)S(1)} %get-tuple-element.288), channel_id=1, source_target_pairs={{0,16},{16,32},{32,48},{48,64},{64,80},{80,96},{96,112},{1,17},{17... | collective-permute-start | bytes 786440 | tf_op jit(solution)/shard_map/while/body/eval_jaxpr/ppermute | solution.py:12
  598.9 8.4 %collective-permute-start = (f32[128,512]{1,0:T(8,128)S(1)}, f32[128,512]{1,0:T(8,128)S(1)}, u32[]{:S(2)}, u32[]{:S(2)}) collective-permute-start(f32[128,512]{1,0:T(8,128)S(1)} %slice.40), channel_id=1, source_target_pairs={{16,0},{32,16},{48,32},{64,48},{80,64},{96,80},{112,96},{17,1},{33... | collective-permute-start | bytes 786440 | tf_op jit(solution)/shard_map/while/body/eval_jaxpr/ppermute | solution.py:12
  621.7 10.4 %collective-permute-start.1 = (f32[128,512]{1,0:T(8,128)S(1)}, f32[128,512]{1,0:T(8,128)S(1)}, u32[]{:S(2)}, u32[]{:S(2)}) collective-permute-start(f32[128,512]{1,0:T(8,128)S(1)} %get-tuple-element.288), channel_id=1, source_target_pairs={{0,16},{16,32},{32,48},{48,64},{64,80},{80,96},{96,112},{1,17},{17... | collective-permute-start | bytes 786440 | tf_op jit(solution)/shard_map/while/body/eval_jaxpr/ppermute | solution.py:12
  633.8 10.2 %collective-permute-start = (f32[128,512]{1,0:T(8,128)S(1)}, f32[128,512]{1,0:T(8,128)S(1)}, u32[]{:S(2)}, u32[]{:S(2)}) collective-permute-start(f32[128,512]{1,0:T(8,128)S(1)} %slice.40), channel_id=1, source_target_pairs={{16,0},{32,16},{48,32},{64,48},{80,64},{96,80},{112,96},{17,1},{33... | collective-permute-start | bytes 786440 | tf_op jit(solution)/shard_map/while/body/eval_jaxpr/ppermute | solution.py:12
  645.0 22.2 %collective-permute-start.1 = (f32[128,512]{1,0:T(8,128)S(1)}, f32[128,512]{1,0:T(8,128)S(1)}, u32[]{:S(2)}, u32[]{:S(2)}) collective-permute-start(f32[128,512]{1,0:T(8,128)S(1)} %get-tuple-element.288), channel_id=1, source_target_pairs={{0,16},{16,32},{32,48},{48,64},{64,80},{80,96},{96,112},{1,17},{17... | collective-permute-start | bytes 786440 | tf_op jit(solution)/shard_map/while/body/eval_jaxpr/ppermute | solution.py:12
  668.9 8.7 %collective-permute-start = (f32[128,512]{1,0:T(8,128)S(1)}, f32[128,512]{1,0:T(8,128)S(1)}, u32[]{:S(2)}, u32[]{:S(2)}) collective-permute-start(f32[128,512]{1,0:T(8,128)S(1)} %slice.40), channel_id=1, source_target_pairs={{16,0},{32,16},{48,32},{64,48},{80,64},{96,80},{112,96},{17,1},{33... | collective-permute-start | bytes 786440 | tf_op jit(solution)/shard_map/while/body/eval_jaxpr/ppermute | solution.py:12
  692.0 8.3 %collective-permute-start.1 = (f32[128,512]{1,0:T(8,128)S(1)}, f32[128,512]{1,0:T(8,128)S(1)}, u32[]{:S(2)}, u32[]{:S(2)}) collective-permute-start(f32[128,512]{1,0:T(8,128)S(1)} %get-tuple-element.288), channel_id=1, source_target_pairs={{0,16},{16,32},{32,48},{48,64},{64,80},{80,96},{96,112},{1,17},{17... | collective-permute-start | bytes 786440 | tf_op jit(solution)/shard_map/while/body/eval_jaxpr/ppermute | solution.py:12
Sparse Core Ops, SparseCore 0:
  11.4 65.3 all-gather.1
where the time goes:
time: 721 us; the launch traced here: 708 us
  waiting for transfers between devices  372 us (52%)
  starting transfers between devices  146 us (20%)
  matrix products  68.5 us (10%)
  local copies, waits for them, and re-layouts  64.8 us (9%)
  blocking collectives  23 us (3%)
  other arithmetic  16.9 us (2%)
  between operations  13.6 us (2%)
    ppermute x36, waiting for transfers between devices, shifted(): return lax.ppermute(block, axis, route)  330 us
    ppermute x36, starting transfers between devices, shifted(): return lax.ppermute(block, axis, route)  146 us
    all_gather x1, waiting for transfers between devices, per_device(): lax.all_gather(mirror_entries, 'col', axis=2, tiled=True)  42 us
    dot_general x6, matrix products, apply_block(): lax.dot_general(mirror_directions, mixed_terms, (((0,), (0,)), ((), ())),...  29.9 us
    dot_general x6, matrix products, apply_block(): jnp.dot(mirror_directions, window, precision=PRECISE, preferred_element_t...  23.3 us
    all_gather x1, blocking collectives, per_device(): lax.all_gather(tau_coefficients, 'col', axis=2, tiled=True)  23 us
    slice x18, local copies, waits for them, and re-layouts, advance(): below_rows = shifted(current[:width_rows], 'row', -1)  17.4 us
    cond x6, local copies, waits for them, and re-layouts  15.8 us
  transfers between devices with their start and end apart: 37, of which 37 were waited for; matrix products, arithmetic and copies ran while one was open for 0% of the time, Pallas kernels for 0%

commit v1 on v0

v1 whole, which is shorter than its diff:
```python
import jax
import jax.numpy as jnp
from jax import lax
from jax.experimental import pallas as pl
from jax.experimental.pallas import tpu as pltpu
from jax.sharding import PartitionSpec as P

EXACT = lax.Precision.HIGHEST
THREE = lax.Precision.HIGH
MESH = pl.DeviceIdType.MESH
B = 128
NC = 4


def mm(a, b, precision, ca=1, cb=0):
    return lax.dot_general(
        a, b, (((ca,), (cb,)), ((), ())), precision=precision, preferred_element_type=jnp.float32
    )


def bmm(a, b, ca=2, cb=1):
    return lax.dot_general(
        a, b, (((ca,), (cb,)), ((0,), (0,))), precision=EXACT, preferred_element_type=jnp.float32
    )


def factors_of(gram, scale, live):
    diag = jnp.where(live, scale, jnp.ones_like(scale))
    power = -(diag[:, :, None] * jnp.triu(gram, 1))
    order = gram.shape[1]
    inverse = jnp.eye(order, dtype=jnp.float32)[None] + power
    reached = 1
    while 2 * reached < order:
        power = bmm(power, power)
        inverse = inverse + bmm(inverse, power)
        reached = reached * 2
    return inverse * diag[:, None, :]


def chain_kernel(
    xh, pm, gc, tb, e, f, c_out, head_out, y, ty, hin, hout, xs, own, s_up0, s_up, s_dn, r_h, r_t
):
    groups = pm.shape[0]
    width = hin.shape[-1]
    chunks = hin.shape[1]
    row = lax.axis_index("row")
    rows = lax.axis_size("row")
    first = row == 0
    last = row == rows - 1

    bar = pltpu.get_barrier_semaphore()

    @pl.when(jnp.logical_not(first))
    def _():
        pl.semaphore_signal(bar, inc=1, device_id={"row": row - 1}, device_id_type=MESH)

    @pl.when(jnp.logical_not(last))
    def _():
        pl.semaphore_signal(bar, inc=1, device_id={"row": row + 1}, device_id_type=MESH)

    @pl.when(first | last)
    def _():
        pl.semaphore_wait(bar, 1)

    @pl.when(jnp.logical_not(first | last))
    def _():
        pl.semaphore_wait(bar, 2)

    def up0(k):
        return pltpu.make_async_remote_copy(
            src_ref=xs.at[k],
            dst_ref=hin.at[0, k, pl.ds(B, B)],
            send_sem=s_up0.at[k],
            recv_sem=r_t.at[0, k],
            device_id={"row": row - 1},
            device_id_type=MESH,
        )

    def up(g, k):
        return pltpu.make_async_remote_copy(
            src_ref=hout.at[g, k, pl.ds(0, B)],
            dst_ref=hin.at[g + 1, k, pl.ds(B, B)],
            send_sem=s_up.at[g, k],
            recv_sem=r_t.at[g + 1, k],
            device_id={"row": row - 1},
            device_id_type=MESH,
        )

    def down(g, k):
        return pltpu.make_async_remote_copy(
            src_ref=hout.at[g, k, pl.ds(B, B)],
            dst_ref=hin.at[g, k, pl.ds(0, B)],
            send_sem=s_dn.at[g, k],
            recv_sem=r_h.at[g, k],
            device_id={"row": row + 1},
            device_id_type=MESH,
        )

    def recv_h(g, k):
        return pltpu.make_async_remote_copy(
            src_ref=hout.at[g, k, pl.ds(B, B)],
            dst_ref=hin.at[g, k, pl.ds(0, B)],
            send_sem=s_dn.at[g, k],
            recv_sem=r_h.at[g, k],
            device_id={"row": row - 1},
            device_id_type=MESH,
        )

    def recv_t(g, k):
        return pltpu.make_async_remote_copy(
            src_ref=xs.at[k],
            dst_ref=hin.at[g, k, pl.ds(B, B)],
            send_sem=s_up0.at[k],
            recv_sem=r_t.at[g, k],
            device_id={"row": row + 1},
            device_id_type=MESH,
        )

    for k in range(chunks):
        xs[k] = xh[:, k * width : (k + 1) * width]
        own[k] = xs[k]

    @pl.when(jnp.logical_not(first))
    def _():
        for k in range(chunks):
            up0(k).start()

    @pl.when(last)
    def _():
        for g in range(groups):
            for k in range(chunks):
                hin[g, k, B:] = jnp.zeros((B, width), jnp.float32)

    y[...] = pm[...]
    ty[...] = mm(tb[0], pm[0], THREE)

    def step(g, carry):
        for k in range(chunks):
            cols = slice(k * width, (k + 1) * width)

            @pl.when(jnp.logical_not(first))
            def _():
                recv_h(g, k).wait_recv()

            @pl.when(jnp.logical_not(last))
            def _():
                recv_t(g, k).wait_recv()

            top = jnp.where(first, own[k], hin[g, k, :B])
            h = jnp.concatenate([top, hin[g, k, B:]], axis=0)
            hn = (h - ty[B:, cols]) - mm(f[g], h, THREE)
            hout[g, k] = hn

            @pl.when(jnp.logical_not(last))
            def _():
                down(g, k).start()

            @pl.when(jnp.logical_not(first) & (g < groups - 1))
            def _():
                up(g, k).start()

            own[k] = hn[:B]
            c_out[g, :, cols] = ty[:B, cols] + mm(e[g], h, THREE)

        @pl.when(g < groups - 1)
        def _():
            change = mm(gc[g], c_out[g], THREE)
            y[...] = y[...] - change.reshape(y.shape)
            ty[...] = mm(tb[g + 1], y[g + 1], THREE)

        return carry

    lax.fori_loop(0, groups, step, 0)
    for k in range(chunks):
        head_out[:, k * width : (k + 1) * width] = hout[groups - 1, k, :B]

    @pl.when(jnp.logical_not(first))
    def _():
        for k in range(chunks):
            up0(k).wait_send()

        def drain(g, carry):
            for k in range(chunks):
                up(g, k).wait_send()
            return carry

        lax.fori_loop(0, groups - 1, drain, 0)

    @pl.when(jnp.logical_not(last))
    def _():
        def drain(g, carry):
            for k in range(chunks):
                down(g, k).wait_send()
            return carry

        lax.fori_loop(0, groups, drain, 0)


def chain(xh, pm, gc, tb, e, f):
    groups, _, columns = pm.shape
    width = columns // NC
    vm = pl.BlockSpec(memory_space=pltpu.VMEM)
    f32 = jnp.float32
    return pl.pallas_call(
        chain_kernel,
        out_shape=(
            jax.ShapeDtypeStruct((groups, B, columns), f32),
            jax.ShapeDtypeStruct((B, columns), f32),
        ),
        in_specs=[vm] * 6,
        out_specs=(vm, vm),
        scratch_shapes=[
            pltpu.VMEM((groups, B, columns), f32),
            pltpu.VMEM((3 * B, columns), f32),
            pltpu.VMEM((groups, NC, 2 * B, width), f32),
            pltpu.VMEM((groups, NC, 2 * B, width), f32),
            pltpu.VMEM((NC, B, width), f32),
            pltpu.VMEM((NC, B, width), f32),
            pltpu.SemaphoreType.DMA((NC,)),
            pltpu.SemaphoreType.DMA((groups, NC)),
            pltpu.SemaphoreType.DMA((groups, NC)),
            pltpu.SemaphoreType.DMA((groups, NC)),
            pltpu.SemaphoreType.DMA((groups, NC)),
        ],
        compiler_params=pltpu.CompilerParams(
            collective_id=0, has_side_effects=True, vmem_limit_bytes=40 << 20
        ),
        name="chain",
    )(xh, pm, gc, tb, e, f)


def per_device(x, mirror_entries, tau, tallies):
    v = lax.all_gather(mirror_entries, "col", axis=2, tiled=True)[:, 0]
    scale = lax.all_gather(tau, "col", axis=2, tiled=True)[:, 0]
    counts = tallies[:, 0]
    row_count, columns = x.shape
    groups, width, window = v.shape
    position = lax.axis_index("row")
    sections = lax.axis_size("row")
    live = lax.iota(jnp.int32, width)[None, :] < counts[:, None]
    keep = (lax.iota(jnp.int32, window) < row_count) | (position != sections - 1)
    v = v * live[:, :, None].astype(jnp.float32) * keep[None, None, :].astype(jnp.float32)
    w = jnp.concatenate([v[:, :, :B], v[:, :, row_count:]], axis=2)
    mid = v.reshape(groups * width, window)[:, B:row_count]
    xm = x[B:]
    pm = mm(mid, xm, THREE).reshape(groups, width, columns)
    gm = mm(mid, mid, THREE, 1, 1).reshape(groups, width, groups, width)
    gd = jnp.stack([gm[g, :, g] for g in range(groups)]) + bmm(w, w, 2, 2)
    tf = factors_of(gd, scale, live)
    e = bmm(tf, w)
    b = bmm(w, tf, 1, 1)
    f = bmm(b, w)
    tb = jnp.concatenate([tf, b], axis=1)
    below = jnp.arange(groups)[:, None] > jnp.arange(groups)[None, :]
    gc = jnp.where(below[:, None, :, None], gm, 0.0).transpose(2, 0, 1, 3)
    gc = gc.reshape(groups, groups * width, width)
    c, head = chain(x[:B], pm, gc, tb, e, f)
    out_mid = xm - mm(mid, c.reshape(groups * width, columns), THREE, 0, 0)
    return jnp.concatenate([head, out_mid], axis=0)


def solution(mesh):
    in_specs = (P("row", "col"), P(None, "row", "col", None), P(None, "row", "col"), P(None, "row"))
    return jax.shard_map(
        per_device, mesh=mesh, in_specs=in_specs, out_specs=P("row", "col"), check_vma=False
    )
```

time: 721 us -> 226 us (0.31); the launches traced: 708 us -> 223 us
  waiting for transfers between devices: 372 us -> 41.4 us
  starting transfers between devices: 146 us -> 0.01 us
  Pallas kernels: 0 us -> 96.2 us
  local copies, waits for them, and re-layouts: 64.8 us -> 5.54 us
  matrix products: 68.5 us -> 34.8 us
  other arithmetic: 16.9 us -> 8.62 us
    ppermute x36 -> x0, waiting for transfers between devices: 330 us -> none  [shifted(): return lax.ppermute(block, axis, route)]
    ppermute x36 -> x0, starting transfers between devices: 146 us -> none  [shifted(): return lax.ppermute(block, axis, route)]
    pallas_call x0 -> x1, Pallas kernels: none -> 96.2 us  [chain(): pl.pallas_call(chain_kernel, out_shape=(jax.ShapeDtypeStruct((groups, B,...]
    slice x42 -> x4, local copies, waits for them, and re-layouts: 44 us -> 1.46 us  [the longest x1 0.99 us: per_device(): c, head = chain(x[:B], pm, gc, tb, e, f)]
    dot_general x31 -> x19, matrix products: 68.5 us -> 34.8 us  [the longest x3 23.7 us: mm(): lax.dot_general(a, b, (((ca,), (cb,)), ((), ())), precision=precision, pr...]
    cond x6 -> x0, local copies, waits for them, and re-layouts: 15.8 us -> none
    dynamic_update_slice x18 -> x0, other arithmetic: 13.3 us -> none  [advance(): return lax.dynamic_update_slice_in_dim(current, top_rows, 0, 0)]
  transfers between devices with their start and end apart: 37 -> 1, of which waited for: 37 -> 1; matrix products, arithmetic and copies ran while one was open for 0% -> 2% of each run, Pallas kernels for 0% -> 0%
where the time goes in v1:
time: 226 us; the launch traced here: 223 us
  Pallas kernels  96.2 us (43%)
  waiting for transfers between devices  41.4 us (18%)
  matrix products  34.8 us (15%)
  blocking collectives  23.1 us (10%)
  between operations  13.8 us (6%)
  other arithmetic  8.62 us (4%)
  local copies, waits for them, and re-layouts  5.54 us (2%)
    pallas_call x1, Pallas kernels, chain(): pl.pallas_call(chain_kernel, out_shape=(jax.ShapeDtypeStruct((groups, B,...  96.2 us
    all_gather x1, waiting for transfers between devices, per_device(): v = lax.all_gather(mirror_entries, 'col', axis=2, tiled=True)[:, 0]  40.6 us
    dot_general x3, matrix products, mm(): lax.dot_general(a, b, (((ca,), (cb,)), ((), ())), precision=precision, pr...  23.7 us
    all_gather x1, blocking collectives, per_device(): scale = lax.all_gather(tau, 'col', axis=2, tiled=True)[:, 0]  23.1 us
    dot_general x16, matrix products, bmm(): lax.dot_general(a, b, (((ca,), (cb,)), ((0,), (0,))), precision=EXACT, pr...  11 us
  transfers between devices with their start and end apart: 1, of which 1 were waited for; matrix products, arithmetic and copies ran while one was open for 2% of the time, Pallas kernels for 0%

profile of v1, /device:TPU:102, one launch (start us, length us, event | category | flops | bytes accessed | tf_op | source)
XLA Modules:
  0.0 223.3 jit_solution(16470407792715957013)
XLA Ops:
  6.5 0.0 all-gather.2.cloned.1.call-start
  6.5 0.7 all-gather.2.cloned.1.call-update
  7.3 0.8 copy.31
  8.0 23.1 %all_gather.7 = f32[6,1,128]{0,1,2:T(1,128)S(1)} all-gather(f32[6,1,8]{0,1,2:T(1,128)S(1)} %copy.31), channel_id=1, replica_groups=mesh['row'=8,'col'=16] {'col'}, dimensions={2}, use_global_device_ids=true | all-gather | bytes 3264 | tf_op jit(solution)/shard_map/all_gather | solution.py:234
  31.2 0.1 copy.32
  31.2 0.7 compare_select_fusion
  32.0 0.1 copy.39
  32.0 1.0 slice.33.xh
  33.1 0.7 fusion.29
  33.8 0.7 bitcast_select_fusion
  34.6 40.6 %all-gather.2.cloned.1.call-done = f32[6,1,128,2176]{3,2,0,1:T(8,128)} async-done(((f32[6,1,8,2176]{3,2,0,1:T(8,128)}), f32[6,1,128,2176]{3,2,0,1:T(8,128)}) %all-gather.2.cloned.1.call-update) | async-done | bytes 6684688 | tf_op jit(solution)/shard_map/all_gather | solution.py:233
  75.2 13.2 %fusion.2 = f32[768,768]{1,0:T(8,128)} fusion(f32[768,2176]{1,0:T(8,128)} %bitcast.65, f32[1920]{0:T(1024)S(1)} %slice.45, f32[768]{0:T(1024)S(1)} %get-tuple-element.18), kind=kOutput, calls=%fused_computation.5 | convolution fusion | flops 6797721600 | bytes 8268288 | tf_op jit(solution)/shard_map/dot_general | solution.py:16
  88.3 2.7 %reshape.131 = f32[6,128,6,128]{3,2,1,0:T(8,128)S(1)} reshape(f32[768,768]{1,0:T(8,128)} %fusion.2) | data formatting | bytes 4718592 | tf_op jit(solution)/shard_map/reshape | solution.py:247
  91.0 0.4 fusion.36
  91.5 3.5 %fusion = f32[6,128,2176]{2,1,0:T(8,128)S(1)} fusion(f32[6,1,128,2176]{3,2,0,1:T(8,128)} %all-gather.2.cloned.1.call-done, f32[2176]{0:T(1024)S(1)} %fusion.28, f32[6,128]{1,0:T(8,128)S(1)} %get-tuple-element.17), kind=kLoop, calls=%fused_computation.1 | loop fusion | flops 3342336 | bytes 13381120 | tf_op jit(solution)/shard_map/mul | solution.py:242
  95.0 0.1 fusion.35
  95.1 0.9 fusion.19
  96.0 0.5 fusion.37
  96.5 0.5 fusion.38
  97.0 0.6 convolution_add_fusion.5
  97.6 0.5 fusion.39
  98.1 0.5 convolution_add_fusion.4
  98.6 0.5 fusion.40
  99.2 0.5 convolution_add_fusion.3
  99.7 0.0 slice-start
  99.7 0.5 fusion.41
  100.2 0.5 convolution_add_fusion.2
  100.8 0.5 fusion.42
  101.3 0.5 convolution_add_fusion.1
  101.8 0.5 fusion.20
  102.3 0.0 slice-start.1
  102.4 1.5 fusion.24
  103.9 0.0 copy-start
  103.9 0.8 fusion.23.e
  104.7 1.6 fusion.22.f
  106.3 0.1 pad_maximum_fusion.1.tb
  106.4 0.0 slice-done
  106.4 0.0 slice-done.1
  106.4 0.0 copy-done
  106.4 5.1 %fusion.4 = f32[768,512]{1,0:T(8,128)S(1)} fusion(f32[768,2176]{1,0:T(8,128)S(1)} %bitcast.68, f32[2048,512]{1,0:T(8,128)S(1)} %copy-done, f32[1920]{0:T(1024)S(1)} %slice.45, f32[768]{0:T(1024)S(1)} %get-tuple-element.18), kind=kOutput, calls=%fused_computation.6 | convolution fusion | flops 4532797440 | bytes 11415552 | tf_op jit(solution)/shard_map/dot_general | solution.py:16
  111.6 0.3 select_bitcast_fusion
  111.9 0.5 copy.30
  112.4 0.0 copy-start.1
  112.4 96.2 %chain.1 = (f32[6,128,512]{2,1,0:T(8,128)S(1)}, f32[128,512]{1,0:T(8,128)S(1)}) custom-call(f32[128,512]{1,0:T(8,128)S(1)} %slice.33.xh, f32[6,128,512]{2,1,0:T(8,128)S(1)} %bitcast.64, f32[6,768,128]{2,1,0:T(8,128)S(1)} %bitcast.62, f32[6,384,128]{2,1,0:T(8,128)S(1)} %pad_maximum_fusion.1.tb, f32[6,128,256]{2,1,0:T(8,128)S(1)} %fusion.23.e, ...), custom_call_target="tpu_custom_call" | custom-call | tf_op jit(solution)/shard_map/chain/pallas_call | solution.py:204
  208.6 0.0 copy-done.1
  208.6 5.5 %slice_subtract_fusion = f32[1920,512]{1,0:T(8,128)S(1)} fusion(f32[2048,512]{1,0:T(8,128)S(1)} %copy-done.1, f32[768,512]{1,0:T(8,128)S(1)} %bitcast.63, f32[768,2176]{1,0:T(8,128)S(1)} %bitcast.69, f32[1920]{0:T(1024)S(1)} %slice.45, f32[768]{0:T(1024)S(1)} %get-tuple-element.18), kind=kOutput, calls=%fused_computation.8 | convolution fusion | flops 4533780480 | bytes 15347712 | tf_op jit(solution)/shard_map/dot_general | solution.py:16
  214.0 2.5 %pad_maximum_fusion = f32[2048,512]{1,0:T(8,128)} fusion(f32[1920,512]{1,0:T(8,128)S(1)} %slice_subtract_fusion, f32[128,512]{1,0:T(8,128)S(1)} %get-tuple-element.7), kind=kLoop, calls=%fused_computation.4 | loop fusion | flops 1048576 | bytes 8388608 | tf_op jit(solution)/shard_map/concatenate | solution.py:259
  (12 shorter events, 0.1 us)
Async XLA Ops:
  6.5 68.7 %all-gather.2.cloned.1.call-start = ((), (), s32[]{:S(2)}) async-start(), calls=%async_computation | async-start | bytes 7102464 | tf_op jit(solution)/shard_map/all_gather | solution.py:233
  99.7 6.7 %slice-start = ((s8[6684672]{0:T(1024)(128)(4,1)}), s8[4194304]{0:T(1024)(128)(4,1)S(1)}, s32[]{:S(2)}) async-start(s8[6684672]{0:T(1024)(128)(4,1)} %bitcast.66), calls=%async_computation.1 | async-start | bytes 8388608
  102.3 4.1 %slice-start.1 = ((s8[6684672]{0:T(1024)(128)(4,1)}), s8[2490368]{0:T(1024)(128)(4,1)S(1)}, s32[]{:S(2)}) async-start(s8[6684672]{0:T(1024)(128)(4,1)} %bitcast.66), calls=%async_computation.2 | async-start | bytes 4980736
  103.9 2.6 %copy-start = (f32[2048,512]{1,0:T(8,128)S(1)}, f32[2048,512]{1,0:T(8,128)}, u32[]{:S(2)}) copy-start(f32[2048,512]{1,0:T(8,128)} %param.4) | copy-start | bytes 12582916
  112.4 96.2 %copy-start.1 = (f32[2048,512]{1,0:T(8,128)S(1)}, f32[2048,512]{1,0:T(8,128)}, u32[]{:S(2)}) copy-start(f32[2048,512]{1,0:T(8,128)} %param.4) | copy-start | bytes 12582916
Sparse Core Ops, SparseCore 0:
  9.8 65.3 all-gather.1

commit v2 on v1

--- a/solution.py
+++ b/solution.py
@@ -18,23 +18,252 @@
     )
 
 
-def bmm(a, b, ca=2, cb=1):
-    return lax.dot_general(
-        a, b, (((ca,), (cb,)), ((0,), (0,))), precision=EXACT, preferred_element_type=jnp.float32
-    )
-
-
-def factors_of(gram, scale, live):
-    diag = jnp.where(live, scale, jnp.ones_like(scale))
-    power = -(diag[:, :, None] * jnp.triu(gram, 1))
-    order = gram.shape[1]
-    inverse = jnp.eye(order, dtype=jnp.float32)[None] + power
-    reached = 1
-    while 2 * reached < order:
-        power = bmm(power, power)
-        inverse = inverse + bmm(inverse, power)
-        reached = reached * 2
-    return inverse * diag[:, None, :]
+def mdot(a, b, ca=1, cb=0):
+    return lax.dot_general(a, b, (((ca,), (cb,)), ((), ())), preferred_element_type=jnp.float32)
+
+
+def split(value):
+    high = value.astype(jnp.bfloat16)
+    return high, (value - high.astype(jnp.float32)).astype(jnp.bfloat16)
+
+
+def prep_kernel(
+    vin, live, x, vout, pm, gc, tb, e, f, vbuf, vh, vl, wbuf, gdbuf, xh, xl, s_sem, r_sem, o_sem
+):
+    groups, width, lanes = vbuf.shape
+    window = lanes - B
+    row_count = x.shape[0]
+    half = lanes // 2
+    row, col = lax.axis_index("row"), lax.axis_index("col")
+    keep = (row != lax.axis_size("row") - 1).astype(jnp.float32)
+    side, y, core = col // 8, (col % 8) // 2, col % 2
+
+    def shard(side_, y_):
+        return side_ * 8 + (y_ % 4) * 2 + core
+
+    other = 1 - side
+    to_up = shard(side, y + 1)
+    to_down = shard(side, y + 3)
+    to_x = shard(other, y)
+    to_sib = col + 1 - 2 * core
+
+    bar = pltpu.get_barrier_semaphore()
+    for target in (to_up, to_down, to_x, to_sib):
+        pl.semaphore_signal(bar, inc=1, device_id={"col": target}, device_id_type=MESH)
+
+    def rows_of(owner):
+        return pl.ds(pl.multiple_of(owner * 8, 8), 8)
+
+    for g in range(groups):
+        vbuf[g, rows_of(col), :] = vin[g]
+
+    def copy(g, kind, owner, target, part=None):
+        span = pl.ds(0, lanes) if part is None else pl.ds(part * half, half)
+        place = vbuf.at[g, rows_of(owner), span]
+        return pltpu.make_async_remote_copy(
+            src_ref=place,
+            dst_ref=place,
+            send_sem=s_sem.at[g, kind],
+            recv_sem=r_sem.at[g, kind],
+            device_id={"col": target},
+            device_id_type=MESH,
+        )
+
+    def sent(g, kind):
+        owner, target, part = (
+            (col, to_up, None),
+            (col, to_down, None),
+            (col, to_x, None),
+            (shard(side, y + 3), to_up, 0),
+            (shard(side, y + 1), to_down, 1),
+            (shard(other, y), to_up, None),
+            (shard(other, y), to_down, None),
+            (shard(other, y + 3), to_up, 0),
+            (shard(other, y + 1), to_down, 1),
+        )[kind]
+        return copy(g, kind, owner, target, part)
+
+    def got(g, kind):
+        owner, part = (
+            (shard(side, y + 3), None),
+            (shard(side, y + 1), None),
+            (shard(other, y), None),
+            (shard(side, y + 2), 0),
+            (shard(side, y + 2), 1),
+            (shard(other, y + 3), None),
+            (shard(other, y + 1), None),
+            (shard(other, y + 2), 0),
+            (shard(other, y + 2), 1),
+        )[kind]
+        return copy(g, kind, owner, to_up, part)
+
+    def relay(g, mine, step):
+        owner = shard(side if mine else other, y + step)
+        return copy(g, (9 if mine else 13) + step, owner, to_sib)
+
+    def relayed(g, mine, step):
+        owner = shard(side if mine else other, y + step) + 1 - 2 * core
+        return copy(g, (9 if mine else 13) + step, owner, to_sib)
+
+    def c0(g):
+        for kind in (0, 1, 2):
+            sent(g, kind).start()
+        relay(g, True, 0).start()
+
+    def c1(g):
+        got(g, 0).wait_recv()
+        sent(g, 3).start()
+        relay(g, True, 3).start()
+        got(g, 1).wait_recv()
+        sent(g, 4).start()
+        relay(g, True, 1).start()
+        got(g, 2).wait_recv()
+        sent(g, 5).start()
+        sent(g, 6).start()
+        relay(g, False, 0).start()
+
+    def c2(g):
+        got(g, 5).wait_recv()
+        sent(g, 7).start()
+        relay(g, False, 3).start()
+        got(g, 6).wait_recv()
+        sent(g, 8).start()
+        relay(g, False, 1).start()
+        got(g, 3).wait_recv()
+        got(g, 4).wait_recv()
+        relay(g, True, 2).start()
+
+    def c3(g):
+        got(g, 7).wait_recv()
+        got(g, 8).wait_recv()
+        relay(g, False, 2).start()
+
+    def c4(g):
+        for mine in (True, False):
+            for step in range(4):
+                relayed(g, mine, step).wait_recv()
+        pltpu.make_async_copy(vbuf.at[g], vout.at[g], o_sem.at[g]).start()
+
+    def products(g):
+        alive = live[:, g : g + 1]
+        mid = vbuf[g, :, B:row_count] * alive
+        high, low = split(mid)
+        at = slice(g * width, (g + 1) * width)
+        vh[at] = high
+        vl[at] = low
+        wbuf[g, :, :B] = vbuf[g, :, :B] * alive
+        wbuf[g, :, B:] = vbuf[g, :, row_count:window] * (alive * keep)
+        high, low = vh[at], vl[at]
+        pm[g] = mdot(high, xh[...]) + mdot(low, xh[...]) + mdot(high, xl[...])
+        upto = slice(0, (g + 1) * width)
+        gram = (
+            mdot(high, vh[upto], 1, 1) + mdot(low, vh[upto], 1, 1) + mdot(high, vl[upto], 1, 1)
+        )
+        for j in range(g):
+            gc[j, at] = gram[:, j * width : (j + 1) * width]
+        w = wbuf[g]
+        gdbuf[g] = gram[:, g * width :] + mm(w, w, EXACT, 1, 1)
+
+    def factors(members):
+        row_at = lax.broadcasted_iota(jnp.int32, (width, width), 0)
+        col_at = lax.broadcasted_iota(jnp.int32, (width, width), 1)
+        eye = (row_at == col_at).astype(jnp.float32)
+        power, inverse, diag = {}, {}, {}
+        for g in members:
+            alive = live[:, g : g + 1]
+            diag[g] = vbuf[g, :, window:] * alive + (1.0 - alive)
+            first = jnp.where(col_at > row_at, -(diag[g] * gdbuf[g]), 0.0)
+            inverse[g] = eye + first
+            power[g] = mm(first, first, EXACT)
+        reached = 2
+        while reached < width:
+            for g in members:
+                if 2 * reached < width:
+                    both = jnp.concatenate([power[g], inverse[g]], axis=0)
+                    both = mm(both, power[g], EXACT)
+                    power[g] = both[:width]
+                    inverse[g] = inverse[g] + both[width:]
+                else:
+                    inverse[g] = inverse[g] + mm(inverse[g], power[g], EXACT)
+            reached = reached * 2
+        for g in members:
+            tf = inverse[g] * diag[g].T
+            w = wbuf[g]
+            ew = mm(tf, w, THREE)
+            e[g] = ew
+            tb[g, :width] = tf
+            bf = mm(w.T, jnp.concatenate([tf, ew], axis=1), THREE)
+            tb[g, width:] = bf[:, :width]
+            f[g] = bf[:, width:]
+
+    pl.semaphore_wait(bar, 4)
+    for g in range(3):
+        c0(g)
+    for j in range(groups):
+        gc[j, : (j + 1) * width] = jnp.zeros(((j + 1) * width, width), jnp.float32)
+    high, low = split(x[B:])
+    xh[...] = high
+    xl[...] = low
+    c1(0)
+    c1(1)
+    c2(0)
+    for g in range(groups):
+        if g + 3 < groups:
+            c0(g + 3)
+        if g + 2 < groups:
+            c1(g + 2)
+        if g + 1 < groups:
+            c2(g + 1)
+        c3(g)
+        c4(g)
+        products(g)
+        if g % 2 == 1:
+            factors((g - 1, g))
+    for g in range(groups):
+        pltpu.make_async_copy(vbuf.at[g], vout.at[g], o_sem.at[g]).wait()
+        for kind in range(9):
+            sent(g, kind).wait_send()
+        for mine in (True, False):
+            for step in range(4):
+                relay(g, mine, step).wait_send()
+
+
+def prep(vin, live, x):
+    groups, _, lanes = vin.shape
+    row_count, columns = x.shape
+    mid = row_count - B
+    vm = pl.BlockSpec(memory_space=pltpu.VMEM)
+    f32, b16 = jnp.float32, jnp.bfloat16
+    shape = jax.ShapeDtypeStruct
+    return pl.pallas_call(
+        prep_kernel,
+        out_shape=(
+            shape((groups, B, lanes), f32),
+            shape((groups, B, columns), f32),
+            shape((groups, groups * B, B), f32),
+            shape((groups, 3 * B, B), f32),
+            shape((groups, B, 2 * B), f32),
+            shape((groups, 2 * B, 2 * B), f32),
+        ),
+        in_specs=[vm] * 3,
+        out_specs=(pl.BlockSpec(memory_space=pl.ANY),) + (vm,) * 5,
+        scratch_shapes=[
+            pltpu.VMEM((groups, B, lanes), f32),
+            pltpu.VMEM((groups * B, mid), b16),
+            pltpu.VMEM((groups * B, mid), b16),
+            pltpu.VMEM((groups, B, 2 * B), f32),
+            pltpu.VMEM((groups, B, B), f32),
+            pltpu.VMEM((mid, columns), b16),
+            pltpu.VMEM((mid, columns), b16),
+            pltpu.SemaphoreType.DMA((groups, 17)),
+            pltpu.SemaphoreType.DMA((groups, 17)),
+            pltpu.SemaphoreType.DMA((groups,)),
+        ],
+        compiler_params=pltpu.CompilerParams(
+            collective_id=1, has_side_effects=True, vmem_limit_bytes=56 << 20
+        ),
+        name="prep",
+    )(vin, live, x)
 
 
 def chain_kernel(
@@ -230,32 +459,16 @@
 
 
 def per_device(x, mirror_entries, tau, tallies):
-    v = lax.all_gather(mirror_entries, "col", axis=2, tiled=True)[:, 0]
-    scale = lax.all_gather(tau, "col", axis=2, tiled=True)[:, 0]
-    counts = tallies[:, 0]
     row_count, columns = x.shape
-    groups, width, window = v.shape
-    position = lax.axis_index("row")
-    sections = lax.axis_size("row")
-    live = lax.iota(jnp.int32, width)[None, :] < counts[:, None]
-    keep = (lax.iota(jnp.int32, window) < row_count) | (position != sections - 1)
-    v = v * live[:, :, None].astype(jnp.float32) * keep[None, None, :].astype(jnp.float32)
-    w = jnp.concatenate([v[:, :, :B], v[:, :, row_count:]], axis=2)
-    mid = v.reshape(groups * width, window)[:, B:row_count]
-    xm = x[B:]
-    pm = mm(mid, xm, THREE).reshape(groups, width, columns)
-    gm = mm(mid, mid, THREE, 1, 1).reshape(groups, width, groups, width)
-    gd = jnp.stack([gm[g, :, g] for g in range(groups)]) + bmm(w, w, 2, 2)
-    tf = factors_of(gd, scale, live)
-    e = bmm(tf, w)
-    b = bmm(w, tf, 1, 1)
-    f = bmm(b, w)
-    tb = jnp.concatenate([tf, b], axis=1)
-    below = jnp.arange(groups)[:, None] > jnp.arange(groups)[None, :]
-    gc = jnp.where(below[:, None, :, None], gm, 0.0).transpose(2, 0, 1, 3)
-    gc = gc.reshape(groups, groups * width, width)
+    groups, _, own, window = mirror_entries.shape
+    lane_tau = jnp.broadcast_to(tau[:, 0, :, None], (groups, own, B))
+    vin = jnp.concatenate([mirror_entries[:, 0], lane_tau], axis=2)
+    live = (lax.iota(jnp.int32, B)[:, None] < tallies[:, 0][None, :]).astype(jnp.float32)
+    live = jnp.pad(live, ((0, 0), (0, B - groups)))
+    v, pm, gc, tb, e, f = prep(vin, live, x)
     c, head = chain(x[:B], pm, gc, tb, e, f)
-    out_mid = xm - mm(mid, c.reshape(groups * width, columns), THREE, 0, 0)
+    mid = v.reshape(groups * B, window + B)[:, B:row_count]
+    out_mid = x[B:] - mm(mid, c.reshape(groups * B, columns), THREE, 0, 0)
     return jnp.concatenate([head, out_mid], axis=0)
 
 

time: 226 us -> 179 us (0.79)
  Pallas kernels: 96.2 us -> 159 us
  waiting for transfers between devices: 41.4 us -> 0 us
  matrix products: 34.8 us -> 5.19 us
  blocking collectives: 23.1 us -> 0 us
  between operations: 13.8 us -> 0.06 us
  other arithmetic: 8.62 us -> 5.55 us
  local copies, waits for them, and re-layouts: 5.54 us -> 8.61 us
    pallas_call x0 -> x1, Pallas kernels: none -> 61.9 us  [prep(): pl.pallas_call(prep_kernel, out_shape=(shape((groups, B, lanes), f32), sh...]
    all_gather x1 -> x0, waiting for transfers between devices: 40.6 us -> none  [per_device(): v = lax.all_gather(mirror_entries, 'col', axis=2, tiled=True)[:, 0]]
    all_gather x1 -> x0, blocking collectives: 23.1 us -> none  [per_device(): scale = lax.all_gather(tau, 'col', axis=2, tiled=True)[:, 0]]
    dot_general x3 -> x1, matrix products: 23.7 us -> 5.19 us  [mm(): lax.dot_general(a, b, (((ca,), (cb,)), ((), ())), precision=precision, pr...]
    dot_general x16 -> x0, matrix products: 11 us -> none  [bmm(): lax.dot_general(a, b, (((ca,), (cb,)), ((0,), (0,))), precision=EXACT, pr...]
    unnamed x14 -> x15, local copies, waits for them, and re-layouts: 0.82 us -> 7.57 us
    mul x1 -> x0, other arithmetic: 3.5 us -> none  [per_device(): v * live[:, :, None].astype(jnp.float32)]
    reshape x1 -> x0, local copies, waits for them, and re-layouts: 2.68 us -> none  [per_device(): gm = mm(mid, mid, THREE, 1, 1).reshape(groups, width, groups, width)]
  transfers between devices with their start and end apart: 1 -> 0, of which waited for: 1 -> 0; matrix products, arithmetic and copies ran while one was open for 2% -> 0% of each run, Pallas kernels for 0% -> 0%
where the time goes in v2:
time: 179 us
  Pallas kernels  159 us (89%)
  local copies, waits for them, and re-layouts  8.61 us (5%)
  other arithmetic  5.55 us (3%)
  matrix products  5.19 us (3%)
    pallas_call x1, Pallas kernels, chain(): pl.pallas_call(chain_kernel, out_shape=(jax.ShapeDtypeStruct((groups, B,...  97.3 us
    pallas_call x1, Pallas kernels, prep(): pl.pallas_call(prep_kernel, out_shape=(shape((groups, B, lanes), f32), sh...  61.9 us
    unnamed x15, local copies, waits for them, and re-layouts  7.57 us
    dot_general x1, matrix products, mm(): lax.dot_general(a, b, (((ca,), (cb,)), ((), ())), precision=precision, pr...  5.19 us

profile of v2, /device:TPU:102, one launch (start us, length us, event | category | flops | bytes accessed | tf_op | source)
XLA Modules:
  0.0 178.6 jit_solution(15761611692071778054)
XLA Ops:
  0.0 0.7 copy.7
  0.7 0.7 iota_compare_fusion
  1.4 0.1 broadcast_in_dim.9
  1.4 0.6 pad_convert_fusion.live
  2.1 1.0 slice.9.xh
  3.0 1.8 %pad_maximum_fusion.1.vin = f32[6,8,2304]{2,1,0:T(8,128)} fusion(f32[6,8,128]{2,1,0:T(8,128)S(1)} %broadcast_in_dim.9, f32[6,8,2176]{2,1,0:T(8,128)} %bitcast.10), kind=kLoop, calls=%fused_computation.4 | loop fusion | flops 110592 | bytes 884736 | tf_op jit(solution)/shard_map/concatenate | solution.py:465
  4.8 0.0 copy-start.5
  4.8 61.9 %prep.1 = (f32[6,128,2304]{2,1,0:T(8,128)}, f32[6,128,512]{2,1,0:T(8,128)}, f32[6,768,128]{2,1,0:T(8,128)}, f32[6,384,128]{2,1,0:T(8,128)}, f32[6,128,256]{2,1,0:T(8,128)}, /*index=5*/f32[6,256,256]{2,1,0:T(8,128)}) custom-call(f32[6,8,2304]{2,1,0:T(8,128)} %pad_maximum_fusion.1.vin, f32[128,128]{1,0:T(8,128)} %pad_convert_fusion.live, f32[2048,512]{1,0:T(8,128)} %x.3), custom_call_target="tpu_custom_call" | custom-call | tf_op jit(solution)/shard_map/prep/pallas_call | solution.py:238
  66.7 0.0 copy-start
  66.7 1.7 copy-done
  68.4 0.0 copy-start.1
  68.4 1.4 copy-done.1
  69.8 0.0 copy-start.2
  69.8 1.4 copy-done.2
  71.2 0.0 copy-start.3
  71.2 1.3 copy-done.3
  72.5 0.0 copy-start.4
  72.5 1.1 copy-done.4
  73.6 0.0 copy-start.6
  73.6 97.3 %chain.1 = (f32[6,128,512]{2,1,0:T(8,128)S(1)}, f32[128,512]{1,0:T(8,128)S(1)}) custom-call(f32[128,512]{1,0:T(8,128)S(1)} %slice.9.xh, f32[6,128,512]{2,1,0:T(8,128)S(1)} %copy-done.1, f32[6,768,128]{2,1,0:T(8,128)S(1)} %copy-done, f32[6,384,128]{2,1,0:T(8,128)S(1)} %copy-done.3, f32[6,128,256]{2,1,0:T(8,128)S(1)} %copy-done.4, f32[6,256,256]{2,1,0:T(8,128)S(1)} %copy-done.2), custom_call_target="tpu_custom_call" | custom-call | tf_op jit(solution)/shard_map/chain/pallas_call | solution.py:433
  170.9 0.0 copy-done.5
  170.9 0.0 copy-done.6
  170.9 5.2 %slice_subtract_fusion = f32[1920,512]{1,0:T(8,128)S(1)} fusion(f32[2048,512]{1,0:T(8,128)S(1)} %copy-done.5, f32[768,512]{1,0:T(8,128)S(1)} %bitcast.8, f32[768,2304]{1,0:T(8,128)S(1)} %bitcast.9), kind=kOutput, calls=%fused_computation.3 | convolution fusion | flops 4530831360 | bytes 15335424 | tf_op jit(solution)/shard_map/dot_general | solution.py:16
  176.1 2.5 %pad_maximum_fusion = f32[2048,512]{1,0:T(8,128)} fusion(f32[1920,512]{1,0:T(8,128)S(1)} %slice_subtract_fusion, f32[128,512]{1,0:T(8,128)S(1)} %get-tuple-element.18), kind=kLoop, calls=%fused_computation.2 | loop fusion | flops 1048576 | bytes 8388608 | tf_op jit(solution)/shard_map/concatenate | solution.py:472
Async XLA Ops:
  4.8 166.1 %copy-start.5 = (f32[2048,512]{1,0:T(8,128)S(1)}, f32[2048,512]{1,0:T(8,128)}, u32[]{:S(2)}) copy-start(f32[2048,512]{1,0:T(8,128)} %x.3) | copy-start | bytes 12582916
  66.7 1.7 copy-start
  68.4 1.4 copy-start.1
  69.8 1.4 copy-start.2
  71.2 1.3 copy-start.3
  72.5 1.1 copy-start.4
  73.6 97.3 %copy-start.6 = (f32[6,128,2304]{2,1,0:T(8,128)S(1)}, f32[6,128,2304]{2,1,0:T(8,128)}, u32[]{:S(2)}) copy-start(f32[6,128,2304]{2,1,0:T(8,128)} %get-tuple-element.19) | copy-start | bytes 21233668

commit v3 on v1

v3 whole, which is shorter than its diff:
```python
import jax
import jax.numpy as jnp
from jax import lax
from jax.experimental import pallas as pl
from jax.experimental.pallas import tpu as pltpu
from jax.sharding import PartitionSpec as P

EXACT = lax.Precision.HIGHEST
THREE = lax.Precision.HIGH
MESH = pl.DeviceIdType.MESH
B = 128
NC = 4


def mm(a, b, precision, ca=1, cb=0):
    return lax.dot_general(
        a, b, (((ca,), (cb,)), ((), ())), precision=precision, preferred_element_type=jnp.float32
    )


def mdot(a, b, ca=1, cb=0):
    return lax.dot_general(a, b, (((ca,), (cb,)), ((), ())), preferred_element_type=jnp.float32)


def split(value):
    high = value.astype(jnp.bfloat16)
    return high, (value - high.astype(jnp.float32)).astype(jnp.bfloat16)


def fused_kernel(
    vin, ltau, counts, xhbm, vh_out, vl_out, c_out, head_out, x, vbuf, vh, vl, wbuf, xh, xl, pm, grow, tb, e, f,
    ty, hin, hout, xs, own, s_sem, r_sem, o_sem, x_sem, s_up0, s_up, s_dn, r_h, r_t
):
    chunks, part = hin.shape[1], hin.shape[3]
    groups, width, lanes = vbuf.shape
    window = lanes - B
    row_count = x.shape[0]
    half = lanes // 2
    row, col = lax.axis_index("row"), lax.axis_index("col")
    rows = lax.axis_size("row")
    first, last = row == 0, row == rows - 1
    keep = (row != rows - 1).astype(jnp.float32)
    side, yy, core = col // 8, (col % 8) // 2, col % 2

    def shard(side_, y_):
        return side_ * 8 + (y_ % 4) * 2 + core

    other = 1 - side
    to_up = shard(side, yy + 1)
    to_down = shard(side, yy + 3)
    to_x = shard(other, yy)
    to_sib = col + 1 - 2 * core

    x_copy = pltpu.make_async_copy(xhbm, x, x_sem)
    x_copy.start()
    bar = pltpu.get_barrier_semaphore()
    for target in (to_up, to_down, to_x, to_sib):
        pl.semaphore_signal(bar, inc=1, device_id={"col": target}, device_id_type=MESH)

    @pl.when(jnp.logical_not(first))
    def _():
        pl.semaphore_signal(bar, inc=1, device_id={"row": row - 1}, device_id_type=MESH)

    @pl.when(jnp.logical_not(last))
    def _():
        pl.semaphore_signal(bar, inc=1, device_id={"row": row + 1}, device_id_type=MESH)

    def rows_of(owner):
        return pl.ds(pl.multiple_of(owner * 8, 8), 8)

    for g in range(groups):
        vbuf[g, rows_of(col), :window] = vin[g, 0]
        vbuf[g, rows_of(col), window:] = jnp.broadcast_to(ltau[g], (8, B))

    def copy(g, kind, owner, target, part=None):
        span = pl.ds(0, lanes) if part is None else pl.ds(part * half, half)
        place = vbuf.at[g, rows_of(owner), span]
        return pltpu.make_async_remote_copy(
            src_ref=place,
            dst_ref=place,
            send_sem=s_sem.at[g, kind],
            recv_sem=r_sem.at[g, kind],
            device_id={"col": target},
            device_id_type=MESH,
        )

    def sent(g, kind):
        owner, target, part = (
            (col, to_up, None),
            (col, to_down, None),
            (col, to_x, None),
            (shard(side, yy + 3), to_up, 0),
            (shard(side, yy + 1), to_down, 1),
            (shard(other, yy), to_up, None),
            (shard(other, yy), to_down, None),
            (shard(other, yy + 3), to_up, 0),
            (shard(other, yy + 1), to_down, 1),
        )[kind]
        return copy(g, kind, owner, target, part)

    def got(g, kind):
        owner, part = (
            (shard(side, yy + 3), None),
            (shard(side, yy + 1), None),
            (shard(other, yy), None),
            (shard(side, yy + 2), 0),
            (shard(side, yy + 2), 1),
            (shard(other, yy + 3), None),
            (shard(other, yy + 1), None),
            (shard(other, yy + 2), 0),
            (shard(other, yy + 2), 1),
        )[kind]
        return copy(g, kind, owner, to_up, part)

    def relay(g, mine, step):
        owner = shard(side if mine else other, yy + step)
        return copy(g, (9 if mine else 13) + step, owner, to_sib)

    def relayed(g, mine, step):
        owner = shard(side if mine else other, yy + step) + 1 - 2 * core
        return copy(g, (9 if mine else 13) + step, owner, to_sib)

    def c0(g):
        for kind in (0, 1, 2):
            sent(g, kind).start()
        relay(g, True, 0).start()

    def c1(g):
        got(g, 0).wait_recv()
        sent(g, 3).start()
        relay(g, True, 3).start()
        got(g, 1).wait_recv()
        sent(g, 4).start()
        relay(g, True, 1).start()
        got(g, 2).wait_recv()
        sent(g, 5).start()
        sent(g, 6).start()
        relay(g, False, 0).start()

    def c2(g):
        got(g, 5).wait_recv()
        sent(g, 7).start()
        relay(g, False, 3).start()
        got(g, 6).wait_recv()
        sent(g, 8).start()
        relay(g, False, 1).start()
        got(g, 3).wait_recv()
        got(g, 4).wait_recv()
        relay(g, True, 2).start()

    def c3(g):
        got(g, 7).wait_recv()
        got(g, 8).wait_recv()
        relay(g, False, 2).start()

    def c4(g):
        for mine in (True, False):
            for step in range(4):
                relayed(g, mine, step).wait_recv()

    def alive_of(g, size):
        at = lax.broadcasted_iota(jnp.int32, (width, size), 0)
        return (at < counts[g, 0]).astype(jnp.float32)

    def products(g):
        alive = alive_of(g, 1)
        high, low = split(vbuf[g, :, B:row_count] * alive)
        vh[g] = high
        vl[g] = low
        pltpu.make_async_copy(vh.at[g], vh_out.at[g], o_sem.at[g, 0]).start()
        pltpu.make_async_copy(vl.at[g], vl_out.at[g], o_sem.at[g, 1]).start()
        wbuf[g, :, :B] = vbuf[g, :, :B] * alive
        wbuf[g, :, B:] = vbuf[g, :, row_count:window] * (alive * keep)
        pm[g] = mdot(high, xh[...]) + mdot(low, xh[...]) + mdot(high, xl[...])

    def grams(g):
        high, low = vh[g], vl[g]
        allh = vh[...].reshape(groups * width, row_count - B)
        alll = vl[...].reshape(groups * width, row_count - B)
        grow[g] = mdot(high, allh, 1, 1) + mdot(low, allh, 1, 1) + mdot(high, alll, 1, 1)

    def factors(g):
        row_at = lax.broadcasted_iota(jnp.int32, (width, width), 0)
        col_at = lax.broadcasted_iota(jnp.int32, (width, width), 1)
        eye = (row_at == col_at).astype(jnp.float32)
        alive = alive_of(g, width)
        w = wbuf[g]
        here = pl.ds(pl.multiple_of(g * width, width), width)
        gram = grow[g, :, here] + mm(w, w, EXACT, 1, 1)
        grow[g, :, here] = jnp.zeros((width, width), jnp.float32)
        diag = vbuf[g, :, window:] * alive + (1.0 - alive)
        power = jnp.where(col_at > row_at, -(diag * gram), 0.0)
        inverse = eye + power
        power = mm(power, power, EXACT)
        reached = 2
        while reached < width:
            if 2 * reached < width:
                both = mm(jnp.concatenate([power, inverse], axis=0), power, EXACT)
                power = both[:width]
                inverse = inverse + both[width:]
            else:
                inverse = inverse + mm(inverse, power, EXACT)
            reached = reached * 2
        tf = inverse * diag.T
        ew = mm(tf, w, THREE)
        e[g] = ew
        tb[g, :width] = tf
        bf = mm(w.T, jnp.concatenate([tf, ew], axis=1), THREE)
        tb[g, width:] = bf[:, :width]
        f[g] = bf[:, width:]

    @pl.when(first | last)
    def _():
        pl.semaphore_wait(bar, 5)

    @pl.when(jnp.logical_not(first | last))
    def _():
        pl.semaphore_wait(bar, 6)

    c0(0)
    c0(1)
    vh[...] = jnp.zeros_like(vh)
    vl[...] = jnp.zeros_like(vl)
    c_out[...] = jnp.zeros_like(c_out)

    def up0(k):
        return pltpu.make_async_remote_copy(
            src_ref=xs.at[k],
            dst_ref=hin.at[0, k, pl.ds(B, B)],
            send_sem=s_up0.at[k],
            recv_sem=r_t.at[0, k],
            device_id={"row": row - 1},
            device_id_type=MESH,
        )

    def up(g, k):
        return pltpu.make_async_remote_copy(
            src_ref=hout.at[g, k, pl.ds(0, B)],
            dst_ref=hin.at[g + 1, k, pl.ds(B, B)],
            send_sem=s_up.at[g, k],
            recv_sem=r_t.at[g + 1, k],
            device_id={"row": row - 1},
            device_id_type=MESH,
        )

    def down(g, k):
        return pltpu.make_async_remote_copy(
            src_ref=hout.at[g, k, pl.ds(B, B)],
            dst_ref=hin.at[g, k, pl.ds(0, B)],
            send_sem=s_dn.at[g, k],
            recv_sem=r_h.at[g, k],
            device_id={"row": row + 1},
            device_id_type=MESH,
        )

    def recv_h(g, k):
        return pltpu.make_async_remote_copy(
            src_ref=hout.at[g, k, pl.ds(B, B)],
            dst_ref=hin.at[g, k, pl.ds(0, B)],
            send_sem=s_dn.at[g, k],
            recv_sem=r_h.at[g, k],
            device_id={"row": row - 1},
            device_id_type=MESH,
        )

    def recv_t(g, k):
        return pltpu.make_async_remote_copy(
            src_ref=xs.at[k],
            dst_ref=hin.at[g, k, pl.ds(B, B)],
            send_sem=s_up0.at[k],
            recv_sem=r_t.at[g, k],
            device_id={"row": row + 1},
            device_id_type=MESH,
        )

    x_copy.wait()
    for k in range(chunks):
        xs[k] = x[:B, k * part : (k + 1) * part]
        own[k] = xs[k]

    @pl.when(jnp.logical_not(first))
    def _():
        for k in range(chunks):
            up0(k).start()

    @pl.when(last)
    def _():
        for g in range(groups):
            for k in range(chunks):
                hin[g, k, B:] = jnp.zeros((B, part), jnp.float32)

    high, low = split(x[B:])
    xh[...] = high
    xl[...] = low
    c1(0)
    c0(2)
    c2(0)
    c1(1)
    lead = jnp.minimum(1 + row // 2, groups)

    def link(g, k):
        cols = slice(k * part, (k + 1) * part)

        @pl.when(jnp.logical_not(first))
        def _():
            recv_h(g, k).wait_recv()

        @pl.when(jnp.logical_not(last))
        def _():
            recv_t(g, k).wait_recv()

        top = jnp.where(first, own[k], hin[g, k, :B])
        h = jnp.concatenate([top, hin[g, k, B:]], axis=0)
        hn = (h - ty[B:, cols]) - mm(f[g], h, THREE)
        hout[g, k] = hn

        @pl.when(jnp.logical_not(last))
        def _():
            down(g, k).start()

        @pl.when(jnp.logical_not(first) & (g < groups - 1))
        def _():
            up(g, k).start()

        own[k] = hn[:B]
        c_out[g, :, cols] = ty[:B, cols] + mm(e[g], h, THREE)

    def step(t, carry):
        @pl.when(t < groups)
        def _():
            c3(t)

        @pl.when(t + 3 < groups)
        def _():
            c0(t + 3)

        @pl.when(t + 1 < groups)
        def _():
            c2(t + 1)

        @pl.when(t + 2 < groups)
        def _():
            c1(t + 2)

        def chain(k):
            @pl.when((t >= lead) & (t < lead + groups))
            def _():
                link(t - lead, k)

        def work(piece):
            @pl.when(t < groups)
            def _():
                piece(t)

        chain(0)
        work(c4)
        work(products)
        chain(1)
        work(grams)
        chain(2)
        work(factors)
        chain(3)

        @pl.when((t >= lead - 1) & (t < lead + groups - 1))
        def _():
            g = t - lead + 1
            whole = c_out[...].reshape(groups * width, c_out.shape[2])
            ty[...] = mm(tb[g], pm[g] - mm(grow[g], whole, THREE), THREE)

        return carry

    lax.fori_loop(0, lead + groups, step, 0)
    for k in range(chunks):
        head_out[:, k * part : (k + 1) * part] = hout[groups - 1, k, :B]

    @pl.when(jnp.logical_not(first))
    def _():
        for k in range(chunks):
            up0(k).wait_send()

        def drain(g, carry):
            for k in range(chunks):
                up(g, k).wait_send()
            return carry

        lax.fori_loop(0, groups - 1, drain, 0)

    @pl.when(jnp.logical_not(last))
    def _():
        def drain(g, carry):
            for k in range(chunks):
                down(g, k).wait_send()
            return carry

        lax.fori_loop(0, groups, drain, 0)

    for g in range(groups):
        pltpu.make_async_copy(vh.at[g], vh_out.at[g], o_sem.at[g, 0]).wait()
        pltpu.make_async_copy(vl.at[g], vl_out.at[g], o_sem.at[g, 1]).wait()
        for kind in range(9):
            sent(g, kind).wait_send()
        for mine in (True, False):
            for step in range(4):
                relay(g, mine, step).wait_send()


def fused(vin, ltau, live, x):
    groups, _, own, window = vin.shape
    lanes = window + B
    row_count, columns = x.shape
    mid = row_count - B
    part = columns // NC
    vm = pl.BlockSpec(memory_space=pltpu.VMEM)
    anywhere = pl.BlockSpec(memory_space=pl.ANY)
    f32, b16 = jnp.float32, jnp.bfloat16
    shape = jax.ShapeDtypeStruct
    dma = pltpu.SemaphoreType.DMA
    return pl.pallas_call(
        fused_kernel,
        out_shape=(
            shape((groups, B, mid), b16),
            shape((groups, B, mid), b16),
            shape((groups, B, columns), f32),
            shape((B, columns), f32),
        ),
        in_specs=[vm, vm, pl.BlockSpec(memory_space=pltpu.SMEM), anywhere],
        out_specs=(anywhere, anywhere, vm, vm),
        scratch_shapes=[
            pltpu.VMEM((row_count, columns), f32),
            pltpu.VMEM((groups, B, lanes), f32),
            pltpu.VMEM((groups, B, mid), b16),
            pltpu.VMEM((groups, B, mid), b16),
            pltpu.VMEM((groups, B, 2 * B), f32),
            pltpu.VMEM((mid, columns), b16),
            pltpu.VMEM((mid, columns), b16),
            pltpu.VMEM((groups, B, columns), f32),
            pltpu.VMEM((groups, B, groups * B), f32),
            pltpu.VMEM((groups, 3 * B, B), f32),
            pltpu.VMEM((groups, B, 2 * B), f32),
            pltpu.VMEM((groups, 2 * B, 2 * B), f32),
            pltpu.VMEM((3 * B, columns), f32),
            pltpu.VMEM((groups, NC, 2 * B, part), f32),
            pltpu.VMEM((groups, NC, 2 * B, part), f32),
            pltpu.VMEM((NC, B, part), f32),
            pltpu.VMEM((NC, B, part), f32),
            dma((groups, 17)),
            dma((groups, 17)),
            dma((groups, 2)),
            dma,
            dma((NC,)),
            dma((groups, NC)),
            dma((groups, NC)),
            dma((groups, NC)),
            dma((groups, NC)),
        ],
        compiler_params=pltpu.CompilerParams(
            collective_id=0, has_side_effects=True, vmem_limit_bytes=60 << 20
        ),
        name="fused",
    )(vin, ltau, live, x)


def finish_kernel(vh_hbm, vl_hbm, c, head, x_hbm, out, x, vh, vl, ch, cl, sem, o_sem):
    pieces, size = x.shape[0], x.shape[1]
    groups, width, _ = vh.shape

    def loads(i):
        cols = pl.ds(i * size, size)
        return (
            pltpu.make_async_copy(x_hbm.at[pl.ds(B + i * size, size)], x.at[i], sem.at[i, 0]),
            pltpu.make_async_copy(vh_hbm.at[:, :, cols], vh.at[:, :, cols], sem.at[i, 1]),
            pltpu.make_async_copy(vl_hbm.at[:, :, cols], vl.at[:, :, cols], sem.at[i, 2]),
        )

    def store(i):
        return pltpu.make_async_copy(x.at[i], out.at[pl.ds(B + i * size, size)], o_sem.at[i])

    for i in range(pieces):
        for load in loads(i):
            load.start()
    top = pltpu.make_async_copy(head, out.at[pl.ds(0, B)], o_sem.at[pieces])
    top.start()
    high, low = split(c[...].reshape(ch.shape))
    ch[...] = high
    cl[...] = low
    for i in range(pieces):
        for load in loads(i):
            load.wait()
        cols = slice(i * size, (i + 1) * size)
        high = vh[:, :, cols].reshape(groups * width, size)
        low = vl[:, :, cols].reshape(groups * width, size)
        change = mdot(high, ch[...], 0, 0) + mdot(low, ch[...], 0, 0) + mdot(high, cl[...], 0, 0)
        x[i] = x[i] - change
        store(i).start()
    top.wait()
    for i in range(pieces):
        store(i).wait()


def finish(vh, vl, c, head, x):
    groups, width, mid = vh.shape
    pieces = 5
    size = mid // pieces
    columns = x.shape[1]
    vm = pl.BlockSpec(memory_space=pltpu.VMEM)
    anywhere = pl.BlockSpec(memory_space=pl.ANY)
    dma = pltpu.SemaphoreType.DMA
    return pl.pallas_call(
        finish_kernel,
        out_shape=jax.ShapeDtypeStruct(x.shape, x.dtype),
        in_specs=[anywhere, anywhere, vm, vm, anywhere],
        out_specs=anywhere,
        scratch_shapes=[
            pltpu.VMEM((pieces, size, columns), jnp.float32),
            pltpu.VMEM(vh.shape, jnp.bfloat16),
            pltpu.VMEM(vh.shape, jnp.bfloat16),
            pltpu.VMEM((groups * width, columns), jnp.bfloat16),
            pltpu.VMEM((groups * width, columns), jnp.bfloat16),
            dma((pieces, 3)),
            dma((pieces + 1,)),
        ],
        compiler_params=pltpu.CompilerParams(vmem_limit_bytes=56 << 20),
        name="finish",
    )(vh, vl, c, head, x)


def per_device(x, mirror_entries, tau, tallies):
    vh, vl, c, head = fused(mirror_entries, tau[:, 0, :, None], tallies, x)
    return finish(vh, vl, c, head, x)


def solution(mesh):
    in_specs = (P("row", "col"), P(None, "row", "col", None), P(None, "row", "col"), P(None, "row"))
    return jax.shard_map(
        per_device, mesh=mesh, in_specs=in_specs, out_specs=P("row", "col"), check_vma=False
    )
```

time: 226 us -> 138 us (0.61)
  waiting for transfers between devices: 41.4 us -> 0 us
  Pallas kernels: 96.2 us -> 134 us
  matrix products: 34.8 us -> 0 us
  blocking collectives: 23.1 us -> 0 us
  between operations: 13.8 us -> 0.17 us
  other arithmetic: 8.62 us -> 0 us
  local copies, waits for them, and re-layouts: 5.54 us -> 2.72 us
    all_gather x1 -> x0, waiting for transfers between devices: 40.6 us -> none  [per_device(): v = lax.all_gather(mirror_entries, 'col', axis=2, tiled=True)[:, 0]]
    pallas_call x1 -> x2, Pallas kernels: 96.2 us -> 134 us  [the longest x1 124 us: fused(): pl.pallas_call(fused_kernel, out_shape=(shape((groups, B, mid), b16), sha...]
    dot_general x19 -> x0, matrix products: 34.8 us -> none  [the longest x3 23.7 us: mm(): lax.dot_general(a, b, (((ca,), (cb,)), ((), ())), precision=precision, pr...]
    all_gather x1 -> x0, blocking collectives: 23.1 us -> none  [per_device(): scale = lax.all_gather(tau, 'col', axis=2, tiled=True)[:, 0]]
    mul x1 -> x0, other arithmetic: 3.5 us -> none  [per_device(): v * live[:, :, None].astype(jnp.float32)]
    reshape x1 -> x0, local copies, waits for them, and re-layouts: 2.68 us -> none  [per_device(): gm = mm(mid, mid, THREE, 1, 1).reshape(groups, width, groups, width)]
    concatenate x2 -> x0, other arithmetic: 2.53 us -> none  [the longest x1 2.45 us: per_device(): return jnp.concatenate([head, out_mid], axis=0)]
  transfers between devices with their start and end apart: 1 -> 0, of which waited for: 1 -> 0; matrix products, arithmetic and copies ran while one was open for 2% -> 0% of each run, Pallas kernels for 0% -> 0%
where the time goes in v3:
time: 138 us; the launch traced here: 137 us
  Pallas kernels  134 us (97%)
  local copies, waits for them, and re-layouts  2.72 us (2%)
    pallas_call x1, Pallas kernels, fused(): pl.pallas_call(fused_kernel, out_shape=(shape((groups, B, mid), b16), sha...  124 us
    pallas_call x1, Pallas kernels, finish(): pl.pallas_call(finish_kernel, out_shape=jax.ShapeDtypeStruct(x.shape, x.d...  9.63 us

profile of v3, /device:TPU:102, one launch (start us, length us, event | category | flops | bytes accessed | tf_op | source)
XLA Modules:
  0.0 136.9 jit_solution(8548186947662359637)
XLA Ops:
  0.0 1.3 copy.6.counts
  1.3 1.4 %copy.5.ltau = f32[6,8,1]{2,1,0:T(8,128)} copy(f32[6,8,1]{1,2,0:T(1,128)} %bitcast.1) | data formatting | bytes 384 | tf_op jit(solution)/shard_map/broadcast_in_dim;squeeze | solution.py:528
  2.7 124.4 %fused.1 = (bf16[6,128,1920]{2,1,0:T(8,128)(2,1)}, bf16[6,128,1920]{2,1,0:T(8,128)(2,1)}, f32[6,128,512]{2,1,0:T(8,128)}, f32[128,512]{1,0:T(8,128)}) custom-call(f32[6,1,8,2176]{3,2,1,0:T(8,128)} %vin.1, f32[6,8,1]{2,1,0:T(8,128)} %copy.5.ltau, s32[6,1]{1,0:T(8,128)} %copy.6.counts, f32[2048,512]{1,0:T(8,128)} %x_hbm.1), custom_call_target="tpu_custom_call" | custom-call | tf_op jit(solution)/shard_map/fused/pallas_call | solution.py:418
  127.1 9.6 %finish.1 = f32[2048,512]{1,0:T(8,128)} custom-call(bf16[6,128,1920]{2,1,0:T(8,128)(2,1)} %get-tuple-element.9.vh_hbm, bf16[6,128,1920]{2,1,0:T(8,128)(2,1)} %get-tuple-element.10.vl_hbm, f32[6,128,512]{2,1,0:T(8,128)} %get-tuple-element.11.c, f32[128,512]{1,0:T(8,128)} %get-tuple-element.12.head, f32[2048,512]{1,0:T(8,128)} %x_hbm.1), custom_call_target="tpu_custom_call" | custom-call | tf_op jit(solution)/shard_map/finish/pallas_call | solution.py:508

commit v4 on v3

--- a/solution.py
+++ b/solution.py
@@ -28,8 +28,8 @@
 
 
 def fused_kernel(
-    vin, ltau, counts, xhbm, vh_out, vl_out, c_out, head_out, x, vbuf, vh, vl, wbuf, xh, xl, pm, grow, tb, e, f,
-    ty, hin, hout, xs, own, s_sem, r_sem, o_sem, x_sem, s_up0, s_up, s_dn, r_h, r_t
+    vin, ltau, counts, xhbm, x_out, vh_out, vl_out, c_out, head_out, x, cc, vbuf, vh, vl, wbuf, xh, xl, pm, grow, tb, e, f,
+    ty, hin, hout, xs, own, s_sem, r_sem, o_sem, x_sem, xo_sem, s_up0, s_up, s_dn, r_h, r_t
 ):
     chunks, part = hin.shape[1], hin.shape[3]
     groups, width, lanes = vbuf.shape
@@ -68,9 +68,13 @@
     def rows_of(owner):
         return pl.ds(pl.multiple_of(owner * 8, 8), 8)
 
+    eighth = lax.broadcasted_iota(jnp.int32, (8, B), 0)
     for g in range(groups):
         vbuf[g, rows_of(col), :window] = vin[g, 0]
-        vbuf[g, rows_of(col), window:] = jnp.broadcast_to(ltau[g], (8, B))
+        scale = jnp.zeros((8, B), jnp.float32)
+        for i in range(8):
+            scale = jnp.where(eighth == i, ltau[g, 0, i], scale)
+        vbuf[g, rows_of(col), window:] = scale
 
     def copy(g, kind, owner, target, part=None):
         span = pl.ds(0, lanes) if part is None else pl.ds(part * half, half)
@@ -121,7 +125,7 @@
         return copy(g, (9 if mine else 13) + step, owner, to_sib)
 
     def c0(g):
-        for kind in (0, 1, 2):
+        for kind in (0, 1):
             sent(g, kind).start()
         relay(g, True, 0).start()
 
@@ -160,24 +164,31 @@
 
     def alive_of(g, size):
         at = lax.broadcasted_iota(jnp.int32, (width, size), 0)
-        return (at < counts[g, 0]).astype(jnp.float32)
+        return (at < counts[g]).astype(jnp.float32)
 
     def products(g):
         alive = alive_of(g, 1)
         high, low = split(vbuf[g, :, B:row_count] * alive)
         vh[g] = high
         vl[g] = low
-        pltpu.make_async_copy(vh.at[g], vh_out.at[g], o_sem.at[g, 0]).start()
-        pltpu.make_async_copy(vl.at[g], vl_out.at[g], o_sem.at[g, 1]).start()
         wbuf[g, :, :B] = vbuf[g, :, :B] * alive
         wbuf[g, :, B:] = vbuf[g, :, row_count:window] * (alive * keep)
         pm[g] = mdot(high, xh[...]) + mdot(low, xh[...]) + mdot(high, xl[...])
 
     def grams(g):
-        high, low = vh[g], vl[g]
-        allh = vh[...].reshape(groups * width, row_count - B)
-        alll = vl[...].reshape(groups * width, row_count - B)
-        grow[g] = mdot(high, allh, 1, 1) + mdot(low, allh, 1, 1) + mdot(high, alll, 1, 1)
+        def against(count):
+            high, low = vh[g], vl[g]
+            allh = vh[:count].reshape(count * width, row_count - B)
+            alll = vl[:count].reshape(count * width, row_count - B)
+            grow[g, :, : count * width] = (
+                mdot(high, allh, 1, 1) + mdot(low, allh, 1, 1) + mdot(high, alll, 1, 1)
+            )
+
+        for low_g, high_g in ((0, 1), (1, groups // 2), (groups // 2, groups)):
+
+            @pl.when((g >= low_g) & (g < high_g))
+            def _():
+                against(high_g)
 
     def factors(g):
         row_at = lax.broadcasted_iota(jnp.int32, (width, width), 0)
@@ -217,11 +228,14 @@
     def _():
         pl.semaphore_wait(bar, 6)
 
+    sent(0, 2).start()
     c0(0)
+    sent(1, 2).start()
     c0(1)
     vh[...] = jnp.zeros_like(vh)
     vl[...] = jnp.zeros_like(vl)
-    c_out[...] = jnp.zeros_like(c_out)
+    cc[...] = jnp.zeros_like(cc)
+    grow[...] = jnp.zeros_like(grow)
 
     def up0(k):
         return pltpu.make_async_remote_copy(
@@ -283,6 +297,9 @@
         for k in range(chunks):
             up0(k).start()
 
+    for g in range(2, groups):
+        sent(g, 2).start()
+
     @pl.when(last)
     def _():
         for g in range(groups):
@@ -296,6 +313,11 @@
     c0(2)
     c2(0)
     c1(1)
+    x_back = pltpu.make_async_copy(x, x_out, xo_sem)
+    v_back = (
+        pltpu.make_async_copy(vh.at[groups - 1], vh_out, o_sem.at[0]),
+        pltpu.make_async_copy(vl.at[groups - 1], vl_out, o_sem.at[1]),
+    )
     lead = jnp.minimum(1 + row // 2, groups)
 
     def link(g, k):
@@ -323,24 +345,30 @@
             up(g, k).start()
 
         own[k] = hn[:B]
-        c_out[g, :, cols] = ty[:B, cols] + mm(e[g], h, THREE)
+        cc[g, :, cols] = ty[:B, cols] + mm(e[g], h, THREE)
+
+    def update(g, piece):
+        size = (row_count - B) // 5
+        high, low = split(cc[g])
+        at = slice(piece * size, (piece + 1) * size)
+        change = (
+            mdot(vh[g, :, at], high, 0, 0)
+            + mdot(vl[g, :, at], high, 0, 0)
+            + mdot(vh[g, :, at], low, 0, 0)
+        )
+        there = slice(B + piece * size, B + (piece + 1) * size)
+        x[there] = x[there] - change
 
     def step(t, carry):
-        @pl.when(t < groups)
-        def _():
-            c3(t)
-
-        @pl.when(t + 3 < groups)
-        def _():
-            c0(t + 3)
-
-        @pl.when(t + 1 < groups)
-        def _():
-            c2(t + 1)
-
-        @pl.when(t + 2 < groups)
-        def _():
-            c1(t + 2)
+        def comm(move, g):
+            @pl.when(g < groups)
+            def _():
+                move(g)
+
+        comm(c3, t)
+        comm(c0, t + 3)
+        comm(c2, t + 1)
+        comm(c1, t + 2)
 
         def chain(k):
             @pl.when((t >= lead) & (t < lead + groups))
@@ -352,24 +380,55 @@
             def _():
                 piece(t)
 
+        def spread(*pieces):
+            @pl.when((t > lead) & (t < lead + groups) & ((t >= groups) | (lead == 4)))
+            def _():
+                for piece in pieces:
+                    update(t - lead - 1, piece)
+
         chain(0)
         work(c4)
         work(products)
+        spread(0, 1)
         chain(1)
         work(grams)
+        spread(2, 3)
         chain(2)
+        spread(4)
+
+        @pl.when(t == lead + groups - 1)
+        def _():
+            for back in v_back:
+                back.start()
+
+        @pl.when((t == lead + groups - 1) & (lead == 4))
+        def _():
+            x_back.start()
+
         work(factors)
         chain(3)
 
         @pl.when((t >= lead - 1) & (t < lead + groups - 1))
         def _():
             g = t - lead + 1
-            whole = c_out[...].reshape(groups * width, c_out.shape[2])
+            whole = cc[...].reshape(groups * width, cc.shape[2])
             ty[...] = mm(tb[g], pm[g] - mm(grow[g], whole, THREE), THREE)
 
         return carry
 
     lax.fori_loop(0, lead + groups, step, 0)
+
+    @pl.when(lead < 4)
+    def _():
+        def later(g, carry):
+            for piece in range(5):
+                update(g, piece)
+            return carry
+
+        lax.fori_loop(0, groups - 1 - lead, later, 0)
+        x_back.start()
+
+    c_out[...] = cc[groups - 1]
     for k in range(chunks):
         head_out[:, k * part : (k + 1) * part] = hout[groups - 1, k, :B]
 
@@ -394,9 +453,10 @@
 
         lax.fori_loop(0, groups, drain, 0)
 
+    x_back.wait()
+    for back in v_back:
+        back.wait()
     for g in range(groups):
-        pltpu.make_async_copy(vh.at[g], vh_out.at[g], o_sem.at[g, 0]).wait()
-        pltpu.make_async_copy(vl.at[g], vl_out.at[g], o_sem.at[g, 1]).wait()
         for kind in range(9):
             sent(g, kind).wait_send()
         for mine in (True, False):
@@ -412,21 +472,24 @@
     part = columns // NC
     vm = pl.BlockSpec(memory_space=pltpu.VMEM)
     anywhere = pl.BlockSpec(memory_space=pl.ANY)
+    small = pl.BlockSpec(memory_space=pltpu.SMEM)
     f32, b16 = jnp.float32, jnp.bfloat16
     shape = jax.ShapeDtypeStruct
     dma = pltpu.SemaphoreType.DMA
     return pl.pallas_call(
         fused_kernel,
         out_shape=(
-            shape((groups, B, mid), b16),
-            shape((groups, B, mid), b16),
-            shape((groups, B, columns), f32),
+            shape((row_count, columns), f32),
+            shape((B, mid), b16),
+            shape((B, mid), b16),
+            shape((B, columns), f32),
             shape((B, columns), f32),
         ),
-        in_specs=[vm, vm, pl.BlockSpec(memory_space=pltpu.SMEM), anywhere],
-        out_specs=(anywhere, anywhere, vm, vm),
+        in_specs=[vm, small, small, anywhere],
+        out_specs=(anywhere, anywhere, anywhere, vm, vm),
         scratch_shapes=[
             pltpu.VMEM((row_count, columns), f32),
+            pltpu.VMEM((groups, B, columns), f32),
             pltpu.VMEM((groups, B, lanes), f32),
             pltpu.VMEM((groups, B, mid), b16),
             pltpu.VMEM((groups, B, mid), b16),
@@ -445,7 +508,8 @@
             pltpu.VMEM((NC, B, part), f32),
             dma((groups, 17)),
             dma((groups, 17)),
-            dma((groups, 2)),
+            dma((2,)),
+            dma,
             dma,
             dma((NC,)),
             dma((groups, NC)),
@@ -462,14 +526,13 @@
 
 def finish_kernel(vh_hbm, vl_hbm, c, head, x_hbm, out, x, vh, vl, ch, cl, sem, o_sem):
     pieces, size = x.shape[0], x.shape[1]
-    groups, width, _ = vh.shape
 
     def loads(i):
         cols = pl.ds(i * size, size)
         return (
             pltpu.make_async_copy(x_hbm.at[pl.ds(B + i * size, size)], x.at[i], sem.at[i, 0]),
-            pltpu.make_async_copy(vh_hbm.at[:, :, cols], vh.at[:, :, cols], sem.at[i, 1]),
-            pltpu.make_async_copy(vl_hbm.at[:, :, cols], vl.at[:, :, cols], sem.at[i, 2]),
+            pltpu.make_async_copy(vh_hbm.at[:, cols], vh.at[:, cols], sem.at[i, 1]),
+            pltpu.make_async_copy(vl_hbm.at[:, cols], vl.at[:, cols], sem.at[i, 2]),
         )
 
     def store(i):
@@ -480,15 +543,15 @@
             load.start()
     top = pltpu.make_async_copy(head, out.at[pl.ds(0, B)], o_sem.at[pieces])
     top.start()
-    high, low = split(c[...].reshape(ch.shape))
+    high, low = split(c[...])
     ch[...] = high
     cl[...] = low
     for i in range(pieces):
         for load in loads(i):
             load.wait()
         cols = slice(i * size, (i + 1) * size)
-        high = vh[:, :, cols].reshape(groups * width, size)
-        low = vl[:, :, cols].reshape(groups * width, size)
+        high = vh[:, cols]
+        low = vl[:, cols]
         change = mdot(high, ch[...], 0, 0) + mdot(low, ch[...], 0, 0) + mdot(high, cl[...], 0, 0)
         x[i] = x[i] - change
         store(i).start()
@@ -498,7 +561,7 @@
 
 
 def finish(vh, vl, c, head, x):
-    groups, width, mid = vh.shape
+    width, mid = vh.shape
     pieces = 5
     size = mid // pieces
     columns = x.shape[1]
@@ -514,8 +577,8 @@
             pltpu.VMEM((pieces, size, columns), jnp.float32),
             pltpu.VMEM(vh.shape, jnp.bfloat16),
             pltpu.VMEM(vh.shape, jnp.bfloat16),
-            pltpu.VMEM((groups * width, columns), jnp.bfloat16),
-            pltpu.VMEM((groups * width, columns), jnp.bfloat16),
+            pltpu.VMEM((width, columns), jnp.bfloat16),
+            pltpu.VMEM((width, columns), jnp.bfloat16),
             dma((pieces, 3)),
             dma((pieces + 1,)),
         ],
@@ -525,8 +588,8 @@
 
 
 def per_device(x, mirror_entries, tau, tallies):
-    vh, vl, c, head = fused(mirror_entries, tau[:, 0, :, None], tallies, x)
-    return finish(vh, vl, c, head, x)
+    rest, vh, vl, c, head = fused(mirror_entries, tau, tallies[:, 0], x)
+    return finish(vh, vl, c, head, rest)
 
 
 def solution(mesh):

time: 138 us -> 127 us (0.920)
  Pallas kernels: 134 us -> 127 us
  local copies, waits for them, and re-layouts: 2.72 us -> 0 us
    pallas_call x1, Pallas kernels: 9.63 us -> 5.82 us  [finish(): pl.pallas_call(finish_kernel, out_shape=jax.ShapeDtypeStruct(x.shape, x.d...]
    pallas_call x1, Pallas kernels: 124 us -> 121 us  [fused(): pl.pallas_call(fused_kernel, out_shape=(shape((row_count, columns), f32),...]
    another operation x1 -> x0, local copies, waits for them, and re-layouts: 1.39 us -> none  [per_device(): vh, vl, c, head = fused(mirror_entries, tau[:, 0, :, None], tallies, x)]
where the time goes in v4:
time: 127 us
  Pallas kernels  127 us (100%)
    pallas_call x1, Pallas kernels, fused(): pl.pallas_call(fused_kernel, out_shape=(shape((row_count, columns), f32),...  121 us
    pallas_call x1, Pallas kernels, finish(): pl.pallas_call(finish_kernel, out_shape=jax.ShapeDtypeStruct(x.shape, x.d...  5.82 us

profile of v4, /device:TPU:102, one launch (start us, length us, event | category | flops | bytes accessed | tf_op | source)
XLA Modules:
  0.0 126.5 jit_solution(15994629354414938532)
XLA Ops:
  0.0 120.7 %fused.1 = (f32[2048,512]{1,0:T(8,128)}, bf16[128,1920]{1,0:T(8,128)(2,1)}, bf16[128,1920]{1,0:T(8,128)(2,1)}, f32[128,512]{1,0:T(8,128)}, f32[128,512]{1,0:T(8,128)}) custom-call(f32[6,1,8,2176]{3,2,1,0:T(8,128)} %vin.1, f32[6,1,8]{2,1,0:T(1,128)} %ltau.1, s32[6]{0:T(128)} %bitcast.1, f32[2048,512]{1,0:T(8,128)} %xhbm.1), custom_call_target="tpu_custom_call" | custom-call | tf_op jit(solution)/shard_map/fused/pallas_call | solution.py:479
  120.7 5.8 %finish.1 = f32[2048,512]{1,0:T(8,128)} custom-call(bf16[128,1920]{1,0:T(8,128)(2,1)} %get-tuple-element.10.vh_hbm, bf16[128,1920]{1,0:T(8,128)(2,1)} %get-tuple-element.11.vl_hbm, f32[128,512]{1,0:T(8,128)} %get-tuple-element.12.c, f32[128,512]{1,0:T(8,128)} %get-tuple-element.13.head, f32[2048,512]{1,0:T(8,128)} %get-tuple-element.14.x_hbm), custom_call_target="tpu_custom_call" | custom-call | tf_op jit(solution)/shard_map/finish/pallas_call | solution.py:571

commit v5 on v4

--- a/solution.py
+++ b/solution.py
@@ -202,15 +202,15 @@
         diag = vbuf[g, :, window:] * alive + (1.0 - alive)
         power = jnp.where(col_at > row_at, -(diag * gram), 0.0)
         inverse = eye + power
-        power = mm(power, power, EXACT)
+        power = mm(power, power, THREE)
         reached = 2
         while reached < width:
             if 2 * reached < width:
-                both = mm(jnp.concatenate([power, inverse], axis=0), power, EXACT)
+                both = mm(jnp.concatenate([power, inverse], axis=0), power, THREE)
                 power = both[:width]
                 inverse = inverse + both[width:]
             else:
-                inverse = inverse + mm(inverse, power, EXACT)
+                inverse = inverse + mm(inverse, power, THREE)
             reached = reached * 2
         tf = inverse * diag.T
         ew = mm(tf, w, THREE)
@@ -351,11 +351,9 @@
         size = (row_count - B) // 5
         high, low = split(cc[g])
         at = slice(piece * size, (piece + 1) * size)
-        change = (
-            mdot(vh[g, :, at], high, 0, 0)
-            + mdot(vl[g, :, at], high, 0, 0)
-            + mdot(vh[g, :, at], low, 0, 0)
-        )
+        left = jnp.concatenate([vh[g, :, at], vl[g, :, at], vh[g, :, at]], axis=0)
+        right = jnp.concatenate([high, high, low], axis=0)
+        change = mdot(left, right, 0, 0)
         there = slice(B + piece * size, B + (piece + 1) * size)
         x[there] = x[there] - change
 
@@ -552,8 +550,9 @@
         cols = slice(i * size, (i + 1) * size)
         high = vh[:, cols]
         low = vl[:, cols]
-        change = mdot(high, ch[...], 0, 0) + mdot(low, ch[...], 0, 0) + mdot(high, cl[...], 0, 0)
-        x[i] = x[i] - change
+        left = jnp.concatenate([high, low, high], axis=0)
+        right = jnp.concatenate([ch[...], ch[...], cl[...]], axis=0)
+        x[i] = x[i] - mdot(left, right, 0, 0)
         store(i).start()
     top.wait()
     for i in range(pieces):

time: 127 us -> 124 us (0.976)
  Pallas kernels: 127 us -> 124 us
    pallas_call x1, Pallas kernels: 121 us -> 119 us  [fused(): pl.pallas_call(fused_kernel, out_shape=(shape((row_count, columns), f32),...]
where the time goes in v5:
time: 124 us
  Pallas kernels  124 us (100%)
    pallas_call x1, Pallas kernels, fused(): pl.pallas_call(fused_kernel, out_shape=(shape((row_count, columns), f32),...  119 us
    pallas_call x1, Pallas kernels, finish(): pl.pallas_call(finish_kernel, out_shape=jax.ShapeDtypeStruct(x.shape, x.d...  5.32 us

profile of v5, /device:TPU:102, one launch (start us, length us, event | category | flops | bytes accessed | tf_op | source)
XLA Modules:
  0.0 124.0 jit_solution(2029162090373374269)
XLA Ops:
  0.0 118.7 %fused.1 = (f32[2048,512]{1,0:T(8,128)}, bf16[128,1920]{1,0:T(8,128)(2,1)}, bf16[128,1920]{1,0:T(8,128)(2,1)}, f32[128,512]{1,0:T(8,128)}, f32[128,512]{1,0:T(8,128)}) custom-call(f32[6,1,8,2176]{3,2,1,0:T(8,128)} %vin.1, f32[6,1,8]{2,1,0:T(1,128)} %ltau.1, s32[6]{0:T(128)} %bitcast.1, f32[2048,512]{1,0:T(8,128)} %xhbm.1), custom_call_target="tpu_custom_call" | custom-call | tf_op jit(solution)/shard_map/fused/pallas_call | solution.py:477
  118.7 5.3 %finish.1 = f32[2048,512]{1,0:T(8,128)} custom-call(bf16[128,1920]{1,0:T(8,128)(2,1)} %get-tuple-element.10.vh_hbm, bf16[128,1920]{1,0:T(8,128)(2,1)} %get-tuple-element.11.vl_hbm, f32[128,512]{1,0:T(8,128)} %get-tuple-element.12.c, f32[128,512]{1,0:T(8,128)} %get-tuple-element.13.head, f32[2048,512]{1,0:T(8,128)} %get-tuple-element.14.x_hbm), custom_call_target="tpu_custom_call" | custom-call | tf_op jit(solution)/shard_map/finish/pallas_call | solution.py:570

commit v6 on v5

--- a/solution.py
+++ b/solution.py
@@ -173,15 +173,17 @@
         vl[g] = low
         wbuf[g, :, :B] = vbuf[g, :, :B] * alive
         wbuf[g, :, B:] = vbuf[g, :, row_count:window] * (alive * keep)
-        pm[g] = mdot(high, xh[...]) + mdot(low, xh[...]) + mdot(high, xl[...])
+        both = mdot(jnp.concatenate([high, low], axis=0), xh[...])
+        pm[g] = both[:width] + both[width:] + mdot(high, xl[...])
 
     def grams(g):
         def against(count):
             high, low = vh[g], vl[g]
             allh = vh[:count].reshape(count * width, row_count - B)
             alll = vl[:count].reshape(count * width, row_count - B)
+            both = mdot(jnp.concatenate([high, low], axis=0), allh, 1, 1)
             grow[g, :, : count * width] = (
-                mdot(high, allh, 1, 1) + mdot(low, allh, 1, 1) + mdot(high, alll, 1, 1)
+                both[:width] + both[width:] + mdot(high, alll, 1, 1)
             )
 
         for low_g, high_g in ((0, 1), (1, groups // 2), (groups // 2, groups)):
@@ -318,7 +320,7 @@
         pltpu.make_async_copy(vh.at[groups - 1], vh_out, o_sem.at[0]),
         pltpu.make_async_copy(vl.at[groups - 1], vl_out, o_sem.at[1]),
     )
-    lead = jnp.minimum(1 + row // 2, groups)
+    lead = 1 + row // 3
 
     def link(g, k):
         cols = slice(k * part, (k + 1) * part)
@@ -379,7 +381,7 @@
                 piece(t)
 
         def spread(*pieces):
-            @pl.when((t > lead) & (t < lead + groups) & ((t >= groups) | (lead == 4)))
+            @pl.when((t > lead) & (t < lead + groups) & ((t >= groups) | (row >= 6)))
             def _():
                 for piece in pieces:
                     update(t - lead - 1, piece)
@@ -399,7 +401,7 @@
             for back in v_back:
                 back.start()
 
-        @pl.when((t == lead + groups - 1) & (lead == 4))
+        @pl.when((t == lead + groups - 1) & (row >= 6))
         def _():
             x_back.start()
 
@@ -416,7 +418,7 @@
 
     lax.fori_loop(0, lead + groups, step, 0)
 
-    @pl.when(lead < 4)
+    @pl.when(row < 6)
     def _():
         def later(g, carry):
             for piece in range(5):

time: 124 us -> 123 us (level)
  no operation moved by 1% of the time
where the time goes in v6:
time: 123 us
  Pallas kernels  123 us (100%)
    pallas_call x1, Pallas kernels, fused(): pl.pallas_call(fused_kernel, out_shape=(shape((row_count, columns), f32),...  117 us
    pallas_call x1, Pallas kernels, finish(): pl.pallas_call(finish_kernel, out_shape=jax.ShapeDtypeStruct(x.shape, x.d...  5.32 us

profile of v6, /device:TPU:102, one launch (start us, length us, event | category | flops | bytes accessed | tf_op | source)
XLA Modules:
  0.0 122.8 jit_solution(17557292804378624288)
XLA Ops:
  0.0 117.5 %fused.1 = (f32[2048,512]{1,0:T(8,128)}, bf16[128,1920]{1,0:T(8,128)(2,1)}, bf16[128,1920]{1,0:T(8,128)(2,1)}, f32[128,512]{1,0:T(8,128)}, f32[128,512]{1,0:T(8,128)}) custom-call(f32[6,1,8,2176]{3,2,1,0:T(8,128)} %vin.1, f32[6,1,8]{2,1,0:T(1,128)} %ltau.1, s32[6]{0:T(128)} %bitcast.1, f32[2048,512]{1,0:T(8,128)} %xhbm.1), custom_call_target="tpu_custom_call" | custom-call | tf_op jit(solution)/shard_map/fused/pallas_call | solution.py:479
  117.5 5.3 %finish.1 = f32[2048,512]{1,0:T(8,128)} custom-call(bf16[128,1920]{1,0:T(8,128)(2,1)} %get-tuple-element.10.vh_hbm, bf16[128,1920]{1,0:T(8,128)(2,1)} %get-tuple-element.11.vl_hbm, f32[128,512]{1,0:T(8,128)} %get-tuple-element.12.c, f32[128,512]{1,0:T(8,128)} %get-tuple-element.13.head, f32[2048,512]{1,0:T(8,128)} %get-tuple-element.14.x_hbm), custom_call_target="tpu_custom_call" | custom-call | tf_op jit(solution)/shard_map/finish/pallas_call | solution.py:572

commit v7 on v6

--- a/solution.py
+++ b/solution.py
@@ -5,7 +5,6 @@
 from jax.experimental.pallas import tpu as pltpu
 from jax.sharding import PartitionSpec as P
 
-EXACT = lax.Precision.HIGHEST
 THREE = lax.Precision.HIGH
 MESH = pl.DeviceIdType.MESH
 B = 128
@@ -199,7 +198,7 @@
         alive = alive_of(g, width)
         w = wbuf[g]
         here = pl.ds(pl.multiple_of(g * width, width), width)
-        gram = grow[g, :, here] + mm(w, w, EXACT, 1, 1)
+        gram = grow[g, :, here] + mm(w, w, THREE, 1, 1)
         grow[g, :, here] = jnp.zeros((width, width), jnp.float32)
         diag = vbuf[g, :, window:] * alive + (1.0 - alive)
         power = jnp.where(col_at > row_at, -(diag * gram), 0.0)

time: 123 us -> 123 us (level)
  no operation moved by 1% of the time
where the time goes in v7:
time: 123 us
  Pallas kernels  123 us (100%)
    pallas_call x1, Pallas kernels, fused(): pl.pallas_call(fused_kernel, out_shape=(shape((row_count, columns), f32),...  118 us
    pallas_call x1, Pallas kernels, finish(): pl.pallas_call(finish_kernel, out_shape=jax.ShapeDtypeStruct(x.shape, x.d...  5.32 us

profile of v7, /device:TPU:102, one launch (start us, length us, event | category | flops | bytes accessed | tf_op | source)
XLA Modules:
  0.0 123.3 jit_solution(18398040606799828413)
XLA Ops:
  0.0 118.0 %fused.1 = (f32[2048,512]{1,0:T(8,128)}, bf16[128,1920]{1,0:T(8,128)(2,1)}, bf16[128,1920]{1,0:T(8,128)(2,1)}, f32[128,512]{1,0:T(8,128)}, f32[128,512]{1,0:T(8,128)}) custom-call(f32[6,1,8,2176]{3,2,1,0:T(8,128)} %vin.1, f32[6,1,8]{2,1,0:T(1,128)} %ltau.1, s32[6]{0:T(128)} %bitcast.1, f32[2048,512]{1,0:T(8,128)} %xhbm.1), custom_call_target="tpu_custom_call" | custom-call | tf_op jit(solution)/shard_map/fused/pallas_call | solution.py:478
  118.0 5.3 %finish.1 = f32[2048,512]{1,0:T(8,128)} custom-call(bf16[128,1920]{1,0:T(8,128)(2,1)} %get-tuple-element.10.vh_hbm, bf16[128,1920]{1,0:T(8,128)(2,1)} %get-tuple-element.11.vl_hbm, f32[128,512]{1,0:T(8,128)} %get-tuple-element.12.c, f32[128,512]{1,0:T(8,128)} %get-tuple-element.13.head, f32[2048,512]{1,0:T(8,128)} %get-tuple-element.14.x_hbm), custom_call_target="tpu_custom_call" | custom-call | tf_op jit(solution)/shard_map/finish/pallas_call | solution.py:571
